TPU v7x, 256 devices: a whole 4x4x8 slice. The times are simulated.
256 devices in a mesh: shard: 32 (over z, y_hi, core), replica: 8 (over y_lo, x).
Axes of the slice: x: 4, y: 4 (y_hi: 2, y_lo: 2; y = y_hi * 2 + y_lo), z: 8, core: 2. Of those that a mesh axis runs over, the one named last changes fastest.
Arguments:
- grad_vision: bfloat16 [8, 32, 256, 1280], P('replica', 'shard'), may hold values from -6 to 6
- grad_audio: bfloat16 [8, 32, 256, 1280], P('replica', 'shard'), may hold values from -6 to 6
- grad_lm: bfloat16 [8, 32, 256, 8192], P('replica', 'shard'), may hold values from -6 to 6
- master_vision: float32 [256, 1280], P('shard'), may hold values from -0.036 to 0.036
- master_audio: float32 [256, 1280], P('shard'), may hold values from -0.036 to 0.036
- master_lm: float32 [256, 8192], P('shard'), may hold values from -0.036 to 0.036
- moment_vision: float32 [256, 1280], P('shard'), may hold values from -0.018 to 0.018
- moment_audio: float32 [256, 1280], P('shard'), may hold values from -0.018 to 0.018
- moment_lm: float32 [256, 8192], P('shard'), may hold values from -0.018 to 0.018
- second_vision: float32 [256, 1280], P('shard'), may hold values from 1e-05 to 0.0001
- second_audio: float32 [256, 1280], P('shard'), may hold values from 1e-05 to 0.0001
- second_lm: float32 [256, 8192], P('shard'), may hold values from 1e-05 to 0.0001
- step_counts: int32 [3], replicated, may hold values from 1 to 8
Outputs:
- params_vision: bfloat16 [256, 1280], replicated
- params_audio: bfloat16 [256, 1280], replicated
- params_lm: bfloat16 [256, 8192], replicated
- new_master_vision: float32 [256, 1280], P('shard')
- new_master_audio: float32 [256, 1280], P('shard')
- new_master_lm: float32 [256, 8192], P('shard')
- new_moment_vision: float32 [256, 1280], P('shard')
- new_moment_audio: float32 [256, 1280], P('shard')
- new_moment_lm: float32 [256, 8192], P('shard')
- new_second_vision: float32 [256, 1280], P('shard')
- new_second_audio: float32 [256, 1280], P('shard')
- new_second_lm: float32 [256, 8192], P('shard')
All inputs are finite; a program needn't handle non-finite values.
Results may differ from a plain program's by a relative error of at most 0.001.
Values may be sent and summed in bfloat16 or wider, within the bound.
A program may use at most 128 MiB of HBM per device.

v0:
```python
import jax
import jax.numpy as jnp
from jax import lax
from jax.sharding import PartitionSpec as P

BETA_ONE = 0.9
BETA_TWO = 0.95
EPSILON = 1e-08
WEIGHT_DECAY = 0.1
LEARN_RATE = 0.002


def adamw_update(grad_sum, master, moment, second, count, devices_all):
    grad = grad_sum / devices_all
    moment_new = BETA_ONE * moment + (1.0 - BETA_ONE) * grad
    second_new = BETA_TWO * second + (1.0 - BETA_TWO) * grad * grad
    steps = count.astype(jnp.float32)
    first_fix = 1.0 - jnp.power(jnp.float32(BETA_ONE), steps)
    second_fix = 1.0 - jnp.power(jnp.float32(BETA_TWO), steps)
    update = (
        moment_new / first_fix / (jnp.sqrt(second_new / second_fix) + EPSILON)
        + WEIGHT_DECAY * master
    )
    master_new = master - LEARN_RATE * update
    return (master_new, moment_new, second_new)


def update_all(totals, masters, moments, seconds, step_counts, devices_all):
    results = [
        adamw_update(totals[k], masters[k], moments[k], seconds[k], step_counts[k], devices_all)
        for k in range(3)
    ]
    new_masters = tuple((r[0] for r in results))
    new_moments = tuple((r[1] for r in results))
    new_seconds = tuple((r[2] for r in results))
    rounded = tuple((m.astype(jnp.bfloat16) for m in new_masters))
    return (new_masters, new_moments, new_seconds, rounded)


def per_device(
    grad_vision,
    grad_audio,
    grad_lm,
    master_vision,
    master_audio,
    master_lm,
    moment_vision,
    moment_audio,
    moment_lm,
    second_vision,
    second_audio,
    second_lm,
    step_counts,
):
    devices_all = float(lax.axis_size("shard") * lax.axis_size("replica"))
    grads = (grad_vision, grad_audio, grad_lm)
    masters = (master_vision, master_audio, master_lm)
    moments = (moment_vision, moment_audio, moment_lm)
    seconds = (second_vision, second_audio, second_lm)
    terms = tuple((g.reshape(g.shape[2], g.shape[3]).astype(jnp.float32) for g in grads))
    shares = (
        lax.psum_scatter(terms[0], "shard", scatter_dimension=0, tiled=True),
        lax.psum_scatter(terms[1], "shard", scatter_dimension=0, tiled=True),
        lax.psum_scatter(terms[2], "shard", scatter_dimension=0, tiled=True),
    )
    totals = lax.psum((shares[0], shares[1], shares[2]), "replica")
    new_masters, new_moments, new_seconds, rounded = update_all(
        totals, masters, moments, seconds, step_counts, devices_all
    )
    params = (
        lax.all_gather(rounded[0], "shard", axis=0, tiled=True),
        lax.all_gather(rounded[1], "shard", axis=0, tiled=True),
        lax.all_gather(rounded[2], "shard", axis=0, tiled=True),
    )
    return (
        params[0],
        params[1],
        params[2],
        new_masters[0],
        new_masters[1],
        new_masters[2],
        new_moments[0],
        new_moments[1],
        new_moments[2],
        new_seconds[0],
        new_seconds[1],
        new_seconds[2],
    )


def solution(mesh):
    return jax.shard_map(
        per_device,
        mesh=mesh,
        in_specs=(
            P("replica", "shard", None, None),
            P("replica", "shard", None, None),
            P("replica", "shard", None, None),
            P("shard", None),
            P("shard", None),
            P("shard", None),
            P("shard", None),
            P("shard", None),
            P("shard", None),
            P("shard", None),
            P("shard", None),
            P("shard", None),
            P(),
        ),
        out_specs=(
            P(),
            P(),
            P(),
            P("shard", None),
            P("shard", None),
            P("shard", None),
            P("shard", None),
            P("shard", None),
            P("shard", None),
            P("shard", None),
            P("shard", None),
            P("shard", None),
        ),
        check_vma=False,
    )
```

profile of v0, /device:TPU:1, one launch (start us, length us, event | category | flops | bytes accessed | tf_op | source)
XLA Modules:
  0.0 673.0 jit_solution(6209479501359893361)
XLA Ops:
  7.2 0.0 reduce-scatter.8.cloned.1.call-start
  7.2 6.4 bitcast_convert_fusion
  13.7 0.0 copy-start
  13.7 0.0 copy-start.1
  13.7 0.0 reduce-scatter.8.cloned.1.call-update
  13.7 0.0 copy-start.11
  13.7 0.0 copy-start.2
  13.7 0.0 copy-start.3
  13.7 0.0 copy-start.4
  13.7 0.0 copy-start.5
  13.7 0.0 copy-start.6
  13.8 0.0 copy-start.7
  13.8 0.0 reduce-scatter.4.cloned.1.call-start
  13.8 0.9 copy-done
  14.7 1.1 bitcast_convert_fusion.2
  15.9 0.0 copy-start.8
  15.9 0.0 copy-start.9
  15.9 0.0 copy-start.10
  15.9 0.0 reduce-scatter.4.cloned.1.call-update
  15.9 0.0 reduce-scatter.6.cloned.1.call-start
  16.0 0.0 copy-done.1
  16.0 1.2 bitcast_convert_fusion.1
  17.2 0.0 reduce-scatter.6.cloned.1.call-update
  17.2 0.0 all-reduce.4.cloned.1.call-start
  17.3 150.1 %reduce-scatter.8.cloned.1.call-done = f32[8,8192]{1,0:T(8,128)} async-done(((f32[256,8192]{1,0:T(8,128)}), f32[8,8192]{1,0:T(8,128)}) %reduce-scatter.8.cloned.1.call-update) | async-done | bytes 262160 | tf_op jit(solution)/shard_map/reduce_scatter | solution.py:64
  167.4 0.0 all-reduce.4.cloned.1.call-update
  167.4 0.0 all-reduce.6.cloned.1.call-start
  167.4 0.0 copy-done.11
  167.4 0.6 fusion.3
  168.8 116.8 %reduce-scatter.4.cloned.1.call-done = f32[8,1280]{1,0:T(8,128)} async-done(((f32[256,1280]{1,0:T(8,128)}), f32[8,1280]{1,0:T(8,128)}) %reduce-scatter.4.cloned.1.call-update) | async-done | bytes 40976 | tf_op jit(solution)/shard_map/reduce_scatter | solution.py:62
  285.5 118.4 %reduce-scatter.6.cloned.1.call-done = f32[8,1280]{1,0:T(8,128)} async-done(((f32[256,1280]{1,0:T(8,128)}), f32[8,1280]{1,0:T(8,128)}) %reduce-scatter.6.cloned.1.call-update) | async-done | bytes 40976 | tf_op jit(solution)/shard_map/reduce_scatter | solution.py:63
  403.9 0.0 all-reduce.6.cloned.1.call-update
  404.0 0.0 all-gather.2.cloned.1.call-start
  404.0 79.9 %all-reduce.4.cloned.1.call-done = f32[8,8192]{1,0:T(8,128)} async-done(((f32[8,8192]{1,0:T(8,128)}), f32[8,8192]{1,0:T(8,128)}) %all-reduce.4.cloned.1.call-update) | async-done | bytes 262160 | tf_op jit(solution)/shard_map/psum | solution.py:66
  483.9 0.0 copy-done.2
  483.9 0.0 copy-done.3
  483.9 0.0 copy-done.4
  483.9 2.0 fusion
  485.9 0.0 all-gather.2.cloned.1.call-update
  487.4 74.1 %all-reduce.6.cloned.1.call-done = (f32[8,1280]{1,0:T(8,128)}, f32[8,1280]{1,0:T(8,128)}) async-done(((f32[8,1280]{1,0:T(8,128)}, f32[8,1280]{1,0:T(8,128)}), (f32[8,1280]{1,0:T(8,128)}, f32[8,1280]{1,0:T(8,128)})) %all-reduce.6.cloned.1.call-update) | async-done | bytes 81936 | tf_op jit(solution)/shard_map/psum | solution.py:66
  561.5 0.0 copy-done.5
  561.5 0.0 copy-done.6
  561.5 0.0 copy-done.7
  561.5 1.4 fusion.1
  562.9 49.0 %all_gather.10 = bf16[256,1280]{1,0:T(8,128)(2,1)S(1)} all-gather(bf16[8,1280]{1,0:T(8,128)(2,1)S(1)} %get-tuple-element.18), channel_id=1, replica_groups=mesh['shard'=32,'replica'=8] {'shard'}, dimensions={0}, use_global_device_ids=true | all-gather | bytes 675840 | tf_op jit(solution)/shard_map/all_gather | solution.py:72
  611.9 0.0 copy-done.8
  611.9 0.0 copy-done.9
  611.9 0.0 copy-done.10
  611.9 1.4 fusion.2
  613.3 39.2 %all_gather.9 = bf16[256,1280]{1,0:T(8,128)(2,1)S(1)} all-gather(bf16[8,1280]{1,0:T(8,128)(2,1)S(1)} %get-tuple-element.22), channel_id=1, replica_groups=mesh['shard'=32,'replica'=8] {'shard'}, dimensions={0}, use_global_device_ids=true | all-gather | bytes 675840 | tf_op jit(solution)/shard_map/all_gather | solution.py:71
  652.5 7.4 %all-gather.2.cloned.1.call-done = bf16[256,8192]{1,0:T(8,128)(2,1)} async-done(((bf16[8,8192]{1,0:T(8,128)(2,1)}), bf16[256,8192]{1,0:T(8,128)(2,1)}) %all-gather.2.cloned.1.call-update) | async-done | bytes 4194320 | tf_op jit(solution)/shard_map/all_gather | solution.py:73
  659.9 0.8 copy.31
  660.7 0.8 copy.32
  661.5 4.6 copy.33
Async XLA Ops:
  7.2 160.2 %reduce-scatter.8.cloned.1.call-start = ((), (), s32[]{:S(2)}) async-start(), calls=%async_computation.5 | async-start | bytes 8650752 | tf_op jit(solution)/shard_map/reduce_scatter | solution.py:64
  13.7 1.1 copy-start
  13.7 2.3 copy-start.1
  13.7 153.8 %copy-start.11 = (s32[3]{0:T(128)S(1)}, s32[3]{0:T(128)}, u32[]{:S(2)}) copy-start(s32[3]{0:T(128)} %param.25) | copy-start | bytes 40
  13.7 470.2 %copy-start.2 = (f32[8,8192]{1,0:T(8,128)S(1)}, f32[8,8192]{1,0:T(8,128)}, u32[]{:S(2)}) copy-start(f32[8,8192]{1,0:T(8,128)} %param.18) | copy-start | bytes 786436
  13.7 470.2 %copy-start.3 = (f32[8,8192]{1,0:T(8,128)S(1)}, f32[8,8192]{1,0:T(8,128)}, u32[]{:S(2)}) copy-start(f32[8,8192]{1,0:T(8,128)} %param.24) | copy-start | bytes 786436
  13.7 470.2 %copy-start.4 = (f32[8,8192]{1,0:T(8,128)S(1)}, f32[8,8192]{1,0:T(8,128)}, u32[]{:S(2)}) copy-start(f32[8,8192]{1,0:T(8,128)} %param.21) | copy-start | bytes 786436
  13.7 547.7 %copy-start.5 = (f32[8,1280]{1,0:T(8,128)S(1)}, f32[8,1280]{1,0:T(8,128)}, u32[]{:S(2)}) copy-start(f32[8,1280]{1,0:T(8,128)} %param.17) | copy-start | bytes 122884
  13.7 547.7 %copy-start.6 = (f32[8,1280]{1,0:T(8,128)S(1)}, f32[8,1280]{1,0:T(8,128)}, u32[]{:S(2)}) copy-start(f32[8,1280]{1,0:T(8,128)} %param.23) | copy-start | bytes 122884
  13.8 547.7 %copy-start.7 = (f32[8,1280]{1,0:T(8,128)S(1)}, f32[8,1280]{1,0:T(8,128)}, u32[]{:S(2)}) copy-start(f32[8,1280]{1,0:T(8,128)} %param.20) | copy-start | bytes 122884
  13.8 271.8 %reduce-scatter.4.cloned.1.call-start = ((), (), s32[]{:S(2)}) async-start(), calls=%async_computation.3 | async-start | bytes 1351680 | tf_op jit(solution)/shard_map/reduce_scatter | solution.py:62
  15.9 596.0 %copy-start.8 = (f32[8,1280]{1,0:T(8,128)S(1)}, f32[8,1280]{1,0:T(8,128)}, u32[]{:S(2)}) copy-start(f32[8,1280]{1,0:T(8,128)} %param.16) | copy-start | bytes 122884
  15.9 596.0 %copy-start.9 = (f32[8,1280]{1,0:T(8,128)S(1)}, f32[8,1280]{1,0:T(8,128)}, u32[]{:S(2)}) copy-start(f32[8,1280]{1,0:T(8,128)} %param.22) | copy-start | bytes 122884
  15.9 596.0 %copy-start.10 = (f32[8,1280]{1,0:T(8,128)S(1)}, f32[8,1280]{1,0:T(8,128)}, u32[]{:S(2)}) copy-start(f32[8,1280]{1,0:T(8,128)} %param.19) | copy-start | bytes 122884
  15.9 388.0 %reduce-scatter.6.cloned.1.call-start = ((), (), s32[]{:S(2)}) async-start(), calls=%async_computation.4 | async-start | bytes 1351680 | tf_op jit(solution)/shard_map/reduce_scatter | solution.py:63
  17.2 466.7 %all-reduce.4.cloned.1.call-start = ((), (), s32[]{:S(2)}) async-start(), calls=%async_computation.6 | async-start | bytes 524288 | tf_op jit(solution)/shard_map/psum | solution.py:66
  167.4 394.1 %all-reduce.6.cloned.1.call-start = ((), (), s32[]{:S(2)}) async-start(), calls=%async_computation.8 | async-start | bytes 163840 | tf_op jit(solution)/shard_map/psum | solution.py:66
  404.0 255.9 %all-gather.2.cloned.1.call-start = ((), (), s32[]{:S(2)}) async-start(), calls=%async_computation.7 | async-start | bytes 4325376 | tf_op jit(solution)/shard_map/all_gather | solution.py:73
Sparse Core Ops, SparseCore 0:
  13.8 153.5 reduce-scatter.7
  172.0 113.4 reduce-scatter.3
  289.6 114.2 reduce-scatter.5
  406.4 77.4 all-reduce.3
  486.7 74.7 all-reduce.5
  564.7 95.1 all-gather.1
where the time goes:
time: 673 us
  waiting for transfers between devices  547 us (81%)
  blocking collectives  88.1 us (13%)
  between operations  16.4 us (2%)
  other arithmetic  13.7 us (2%)
  local copies, waits for them, and re-layouts  7.88 us (1%)
    psum x2, waiting for transfers between devices, per_device(): totals = lax.psum((shares[0], shares[1], shares[2]), 'replica')  154 us
    reduce_scatter x1, waiting for transfers between devices, per_device(): lax.psum_scatter(terms[2], 'shard', scatter_dimension=0, tiled=True)  150 us
    reduce_scatter x1, waiting for transfers between devices, per_device(): lax.psum_scatter(terms[1], 'shard', scatter_dimension=0, tiled=True)  118 us
    reduce_scatter x1, waiting for transfers between devices, per_device(): lax.psum_scatter(terms[0], 'shard', scatter_dimension=0, tiled=True)  117 us
    all_gather x1, blocking collectives, per_device(): lax.all_gather(rounded[1], 'shard', axis=0, tiled=True)  49 us
    all_gather x1, blocking collectives, per_device(): lax.all_gather(rounded[0], 'shard', axis=0, tiled=True)  39.2 us
  transfers between devices with their start and end apart: 6, of which 6 were waited for; matrix products, arithmetic and copies ran while one was open for 1% of the time, Pallas kernels for 0%

commit v1 on v0

v1 whole, which is shorter than its diff:
```python
import math

import jax
import jax.numpy as jnp
from jax import lax
from jax.experimental import pallas as pl
from jax.experimental.pallas import tpu as pltpu
from jax.sharding import PartitionSpec as P

BETA_ONE = 0.9
BETA_TWO = 0.95
EPSILON = 1e-08
WEIGHT_DECAY = 0.1
LEARN_RATE = 0.002
MESH = pl.DeviceIdType.MESH
N_SEMS = 480


def adamw_update(grad_sum, master, moment, second, steps, devices_all):
    grad = grad_sum * (1.0 / devices_all)
    moment_new = BETA_ONE * moment + (1.0 - BETA_ONE) * grad
    second_new = BETA_TWO * second + (1.0 - BETA_TWO) * grad * grad
    t = jnp.full(grad_sum.shape, steps, jnp.float32)
    first_fix = 1.0 - jnp.exp(t * math.log(BETA_ONE))
    second_fix = 1.0 - jnp.exp(t * math.log(BETA_TWO))
    update = (
        moment_new / first_fix / (jnp.sqrt(second_new / second_fix) + EPSILON)
        + WEIGHT_DECAY * master
    )
    master_new = master - LEARN_RATE * update
    return master_new, moment_new, second_new


def coordinates():
    s, r = lax.axis_index("shard"), lax.axis_index("replica")
    z, yh, c = lax.div(s, 4), lax.rem(lax.div(s, 2), 2), lax.rem(s, 2)
    yl, x = lax.div(r, 4), lax.rem(r, 4)
    return x, yh, yl, z, c


def device(x, y, z, c):
    return (z * 4 + lax.div(y, 2) * 2 + c, lax.rem(y, 2) * 4 + x)


def cols(start, size):
    return pl.ds(pl.multiple_of(start, 128), size)


def step_kernel(
    gv, ga, gl, mv, ma, ml, nv, na, nl, sv, sa_, sl, steps,
    pv, pa, pm, tv, ta, tl,
    own_a, own_b, own_c, got_a, got_b, got_c, sum_a, sum_b, sum_c,
    rm_a, lm_a, b_r2, b_l2, b_from_l, b_from_r, c_r2, c_l2, c_from_l, c_from_r,
    a1, a2_got, a3_all,
    b1, b1_r2, b1_l2, b1_from_l, b1_from_r, b2, b3_got,
    c1, rm_c, lm_c, c2, c3_got,
    st_a, st_b, st_c, totals, all_a, all_b, all_c, sems,
):
    x, yh, yl, z, c = coordinates()
    y = yh * 2 + yl
    other = 1 - c
    f32 = jnp.float32

    def xj(j):
        return lax.rem(x + j, 4)

    def yj(j):
        return lax.rem(y + j, 4)

    def zj(j):
        return lax.rem(z + j, 8)

    core = device(x, y, z, other)
    right_x, left_x = device(xj(1), y, z, c), device(xj(3), y, z, c)
    right_y, left_y = device(x, yj(1), z, c), device(x, yj(3), z, c)
    right_z, left_z = device(x, y, zj(1), c), device(x, y, zj(7), c)
    y_twin = yh * 2 + (1 - yl)

    used = [0]
    started = []

    def sem():
        used[0] += 1
        return sems.at[used[0] - 1]

    def send(src, dst, to):
        copy = pltpu.make_async_remote_copy(
            src_ref=src, dst_ref=dst, send_sem=sem(), recv_sem=sem(),
            device_id=to, device_id_type=MESH,
        )
        copy.start()
        started.append(copy.wait_send)
        return copy

    def load(src, dst):
        copy = pltpu.make_async_copy(src, dst, sem())
        copy.start()
        return copy

    order = [("b", 2), ("c", 2), ("a", 4), ("b", 1), ("c", 1), ("a", 3), ("b", 3), ("c", 3), ("a", 5),
             ("a", 2), ("a", 6), ("a", 1), ("a", 7), ("b", 0), ("c", 0), ("a", 0)]

    def piece(part, j, half):
        if part == "b":
            yy = yj(j)
            at = gl.at[:, lax.div(yy, 2), :, cols(4096 * half + lax.rem(yy, 2) * 1024, 1024)]
            return [(at, lambda own, got: (own_b if own else got_b).at[j])]
        if part == "c":
            at = gl.at[:, :, :, cols(4096 * half + 2048 + xj(j) * 512, 512)]
            return [(at, lambda own, got: (own_c if own else got_c).at[j])]
        zz = zj(j)
        return [
            (gv.at[zz, :, :, cols(640 * half, 640)], lambda own, got: (own_a if own else got_a).at[j, :, :, pl.ds(0, 640)]),
            (ga.at[zz, :, :, cols(640 * half, 640)], lambda own, got: (own_a if own else got_a).at[j, :, :, pl.ds(640, 640)]),
        ]

    own_copies, core_copies = {}, {}
    for part, j in order:
        own_copies[part, j] = [load(src, dst(True, False)) for src, dst in piece(part, j, c)]

    col_a, col_b, col_c = yl * 640, yl * 1024 + x * 256, 2048 + x * 512 + yl * 256
    mine, theirs = pl.ds(pl.multiple_of(c * 8, 8), 8), pl.ds(pl.multiple_of(other * 8, 8), 8)

    def state_pieces(half):
        pairs = []
        for k, (v, a, m) in enumerate(((mv, ma, ml), (nv, na, nl), (sv, sa_, sl))):
            pairs.append((v.at[:, cols(640 * half, 640)], st_a.at[k, 0, mine]))
            pairs.append((a.at[:, cols(640 * half, 640)], st_a.at[k, 1, mine]))
            pairs.append((m.at[:, cols(4096 * half + col_b, 256)], st_b.at[k, mine]))
            pairs.append((m.at[:, cols(4096 * half + col_c, 256)], st_c.at[k, mine]))
        return pairs

    state_copies = [load(src, dst) for src, dst in state_pieces(c)]

    barrier = pltpu.get_barrier_semaphore()
    peers = [core]
    peers += [device(xj(k), y, z, c) for k in range(1, 4)]
    peers += [device(x, yj(k), z, c) for k in range(1, 4)]
    peers += [device(x, y, zj(k), c) for k in range(1, 8)]
    peers += [device(xj(k), y_twin, z, c) for k in range(1, 4)]
    for peer in peers:
        pl.semaphore_signal(barrier, inc=1, device_id=peer, device_id_type=MESH)
    pl.semaphore_wait(barrier, len(peers))

    for part, j in order:
        core_copies[part, j] = [send(src, dst(False, True), core) for src, dst in piece(part, j, other)]
    state_sends = [send(src, dst, core) for src, dst in state_pieces(other)]

    def chip_sum(part, j):
        for copy in own_copies[part, j]:
            copy.wait()
        for copy in core_copies[part, j]:
            copy.wait_recv()
        own, got, total = {"a": (own_a, got_a, sum_a), "b": (own_b, got_b, sum_b), "c": (own_c, got_c, sum_c)}[part]
        if part == "a":
            total[j] = own[j].astype(f32) + got[j].astype(f32)
        else:

            def body(i, _):
                total[j, i] = own[j, i].astype(f32) + got[j, i].astype(f32)
                return 0

            lax.fori_loop(0, 8, body, 0)

    lo, hi = pl.ds(0, 4), pl.ds(4, 4)

    def add_half(total, j, got, first):
        def body(i, _):
            total[j, first + i] = total[j, first + i] + got[i]
            return 0

        lax.fori_loop(0, 4, body, 0)

    class Ring4:
        def __init__(self, total, r2, l2, from_l, from_r, right, left):
            self.total, self.r2, self.l2, self.from_l, self.from_r = total, r2, l2, from_l, from_r
            self.right, self.left = right, left

        def far(self):
            self.c_r2 = send(self.total.at[2, lo], self.r2, self.right)
            self.c_l2 = send(self.total.at[2, hi], self.l2, self.left)

        def near_right(self):
            self.c_r_hi = send(self.total.at[1, hi], self.from_l.at[hi], self.right)

        def near_left(self):
            self.c_l_lo = send(self.total.at[3, lo], self.from_r.at[lo], self.left)

        def pass_on(self):
            self.c_r2.wait_recv()
            add_half(self.total, 1, self.r2, 0)
            self.c_r_lo = send(self.total.at[1, lo], self.from_l.at[lo], self.right)
            self.c_l2.wait_recv()
            add_half(self.total, 3, self.l2, 4)
            self.c_l_hi = send(self.total.at[3, hi], self.from_r.at[hi], self.left)

        def wait(self):
            for copy in (self.c_r_hi, self.c_l_lo, self.c_r_lo, self.c_l_hi):
                copy.wait_recv()

    class Ring8:
        def __init__(self, total, rm, lm, width):
            self.total, self.rm, self.lm = total, rm, lm
            self.h = (pl.ds(0, width), pl.ds(width, width))
            self.r, self.l = {}, {}

        def send_right(self, j, h):
            at = (slice(None), slice(None), self.h[h])
            self.r[j - 1, h] = send(self.total.at[(j,) + at], self.rm.at[(j - 1,) + at], right_z)

        def send_left(self, j, h):
            at = (slice(None), slice(None), self.h[h])
            self.l[j - 1, h] = send(self.total.at[((8 - j) % 8,) + at], self.lm.at[(j - 1,) + at], left_z)

        def step(self, m, h):
            self.r[m, h].wait_recv()
            at = (slice(None), slice(None), self.h[h])
            self.total[(m,) + at] = self.total[(m,) + at] + self.rm[(m,) + at]
            self.send_right(m, h)
            self.l[m, 1 - h].wait_recv()
            at = (slice(None), slice(None), self.h[1 - h])
            self.total[(8 - m,) + at] = self.total[(8 - m,) + at] + self.lm[(m,) + at]
            self.send_left(m, 1 - h)

        def wait(self):
            for h in (0, 1):
                self.r[0, h].wait_recv()
                self.l[0, h].wait_recv()

    ring_b = Ring4(sum_b, b_r2, b_l2, b_from_l, b_from_r, right_y, left_y)
    ring_c = Ring4(sum_c, c_r2, c_l2, c_from_l, c_from_r, right_x, left_x)
    ring_a = Ring8(sum_a, rm_a, lm_a, 640)

    chip_sum("b", 2)
    ring_b.far()
    chip_sum("c", 2)
    ring_c.far()
    chip_sum("a", 4)
    ring_a.send_right(4, 0)
    ring_a.send_left(4, 1)
    chip_sum("b", 1)
    ring_b.near_right()
    chip_sum("c", 1)
    ring_c.near_right()
    chip_sum("a", 3)
    ring_a.send_right(3, 1)
    chip_sum("b", 3)
    ring_b.near_left()
    chip_sum("c", 3)
    ring_c.near_left()
    chip_sum("a", 5)
    ring_a.send_left(3, 0)
    ring_a.step(3, 0)
    chip_sum("a", 2)
    chip_sum("a", 6)
    ring_a.step(2, 1)
    chip_sum("a", 1)
    chip_sum("a", 7)
    ring_b.pass_on()
    ring_c.pass_on()
    ring_a.step(2, 0)
    ring_a.step(1, 1)
    chip_sum("b", 0)
    chip_sum("c", 0)
    chip_sum("a", 0)
    ring_a.step(1, 0)

    ring_a.wait()
    a1[...] = sum_a[0] + rm_a[0] + lm_a[0]
    a2_copies = []
    for k in range(1, 4):
        yy = yj(k)
        src = a1.at[lax.div(yy, 2), :, cols(lax.rem(yy, 2) * 640, 640)]
        a2_copies.append(send(src, a2_got.at[k - 1], device(x, yy, z, c)))

    ring_b.wait()
    ring_b1 = Ring4(b1, b1_r2, b1_l2, b1_from_l, b1_from_r, right_x, left_x)

    def take_b(j):
        at = cols(xj(j) * 256, 256)

        def body(i, _):
            b1[j, i] = sum_b[0, i, :, at] + b_from_l[i, :, at] + b_from_r[i, :, at]
            return 0

        lax.fori_loop(0, 8, body, 0)

    take_b(2)
    ring_b1.far()
    take_b(1)
    ring_b1.near_right()
    take_b(3)
    ring_b1.near_left()

    ring_c.wait()
    ring_c1 = Ring8(c1, rm_c, lm_c, 256)

    def take_c(j):
        zz = zj(j)
        c1[j] = sum_c[0, zz] + c_from_l[zz] + c_from_r[zz]

    take_c(4)
    ring_c1.send_right(4, 0)
    ring_c1.send_left(4, 1)
    take_c(3)
    ring_c1.send_right(3, 1)
    take_c(5)
    ring_c1.send_left(3, 0)
    take_b(0)

    for copy in a2_copies:
        copy.wait_recv()
    a3_all[x] = a1[yh, :, cols(yl * 640, 640)] + a2_got[0] + a2_got[1] + a2_got[2]
    a3_copies = [send(a3_all.at[x], a3_all.at[x], device(xj(k), y, z, c)) for k in range(1, 4)]

    ring_c1.step(3, 0)
    take_c(2)
    take_c(6)
    ring_c1.step(2, 1)
    ring_b1.pass_on()
    take_c(1)
    take_c(7)
    ring_c1.step(2, 0)
    take_c(0)
    ring_c1.step(1, 1)

    ring_b1.wait()

    def take_b1(i, _):
        b2[i] = b1[0, i] + b1_from_l[i] + b1_from_r[i]
        return 0

    lax.fori_loop(0, 8, take_b1, 0)
    b3_copies = [send(b2.at[zj(k)], b3_got.at[k - 1], device(x, y, zj(k), c)) for k in range(1, 8)]
    ring_c1.step(1, 0)
    ring_c1.wait()
    c2[...] = c1[0] + rm_c[0] + lm_c[0]
    c3_copies = []
    for k in range(1, 4):
        yy = yj(k)
        src = c2.at[lax.div(yy, 2), :, cols(lax.rem(yy, 2) * 256, 256)]
        c3_copies.append(send(src, c3_got.at[k - 1], device(x, yy, z, c)))

    for copy in state_copies:
        copy.wait()
    for copy in state_sends:
        copy.wait_recv()
    t_vision, t_audio, t_lm = (steps[k].astype(f32) for k in range(3))

    for copy in a3_copies:
        copy.wait_recv()
    total_a = (a3_all[0] + a3_all[1]) + (a3_all[2] + a3_all[3])
    totals[:, cols(yl * 640, 640)] = total_a
    t_a = jnp.where(yl == 0, t_vision, t_audio)
    new_a = adamw_update(total_a, st_a[0, yl], st_a[1, yl], st_a[2, yl], t_a, 256.0)[0]
    all_a[z, yh, :, cols(yl * 640, 640)] = new_a.astype(jnp.bfloat16)
    at = all_a.at[z, yh, :, cols(yl * 640, 640)]
    ya_copies = [send(at, at, device(x, yj(k), z, c)) for k in range(1, 4)]

    for copy in b3_copies:
        copy.wait_recv()
    total_b = b2[z]
    for k in range(7):
        total_b = total_b + b3_got[k]
    totals[:, cols(1280 + col_b, 256)] = total_b
    new_b = adamw_update(total_b, st_b[0], st_b[1], st_b[2], t_lm, 256.0)[0]
    all_b[y, z, :, cols(x * 256, 256)] = new_b.astype(jnp.bfloat16)
    at = all_b.at[y, z, :, cols(x * 256, 256)]
    zb_copies = [send(at, at, device(x, y, zj(k), c)) for k in (4, 3, 5, 2, 6, 1, 7)]

    for copy in c3_copies:
        copy.wait_recv()
    total_c = c2[yh, :, cols(yl * 256, 256)] + c3_got[0] + c3_got[1] + c3_got[2]
    totals[:, cols(1280 + col_c, 256)] = total_c
    new_c = adamw_update(total_c, st_c[0], st_c[1], st_c[2], t_lm, 256.0)[0]
    all_c[x, z, yh, :, cols(yl * 256, 256)] = new_c.astype(jnp.bfloat16)
    at = all_c.at[x, z, yh, :, cols(yl * 256, 256)]
    yc_copies = [send(at, at, device(x, yj(k), z, c)) for k in range(1, 4)]

    at_a, at_b, at_c = (totals.at[:, cols(o, w)] for o, w in ((col_a, 640), (1280 + col_b, 256), (1280 + col_c, 256)))
    total_copies = [send(at_a, at_a, device(x, y_twin, z, c))]
    for k in range(4):
        for yy in (y, y_twin):
            if k or yy is not y:
                total_copies.append(send(at_b, at_b, device(xj(k), yy, z, c)))
                total_copies.append(send(at_c, at_c, device(xj(k), yy, z, c)))

    class Gather4:
        def __init__(self, at, right, left, me):
            self.at, self.me = at, me
            self.right, self.left = right, left

        def start(self):
            own = self.at(self.me, None)
            self.r = send(own, own, self.right)
            self.l = send(own, own, self.left)

        def pass_on(self):
            self.r.wait_recv()
            at = self.at(lax.rem(self.me + 3, 4), lo)
            self.r2 = send(at, at, self.right)
            self.l.wait_recv()
            at = self.at(lax.rem(self.me + 1, 4), hi)
            self.l2 = send(at, at, self.left)

        def wait(self):
            self.r2.wait_recv()
            self.l2.wait_recv()

    class Gather8:
        def __init__(self, at):
            self.at = at

        def start(self):
            own = self.at(z, None)
            self.r = send(own, own, right_z)
            self.l = send(own, own, left_z)

        def pass_on(self, k):
            self.r.wait_recv()
            at = self.at(zj(8 - k), 0 if k == 3 else None)
            self.r = send(at, at, right_z)
            self.l.wait_recv()
            at = self.at(zj(k), 1 if k == 3 else None)
            self.l = send(at, at, left_z)

        def wait(self):
            self.r.wait_recv()
            self.l.wait_recv()

    def at_a8(zz, h):
        if h is None:
            return all_a.at[zz]
        return all_a.at[zz, :, :, pl.ds(640 * h, 640)]

    def at_c8(zz, h):
        if h is None:
            return all_c.at[x, zz]
        return all_c.at[x, zz, :, :, pl.ds(256 * h, 256)]

    def at_bx(xx, h):
        return all_b.at[y, slice(None) if h is None else h, :, cols(xx * 256, 256)]

    def at_by(yy, h):
        return all_b.at[yy] if h is None else all_b.at[yy, h]

    def at_cx(xx, h):
        return all_c.at[xx] if h is None else all_c.at[xx, h]

    outs = []

    def put(src, dst):
        outs.append(load(src, dst))
        outs.append(send(src, dst, core))

    def put_b(yy):
        put(all_b.at[yy], pm.at[:, lax.div(yy, 2), :, cols(4096 * c + lax.rem(yy, 2) * 1024, 1024)])

    def put_c(xx):
        put(all_c.at[xx], pm.at[:, :, :, cols(4096 * c + 2048 + xx * 512, 512)])

    gather_a, gather_c = Gather8(at_a8), Gather8(at_c8)
    gather_b, gather_by = Gather4(at_bx, right_x, left_x, x), Gather4(at_by, right_y, left_y, y)
    gather_cx = Gather4(at_cx, right_x, left_x, x)

    for copy in ya_copies:
        copy.wait_recv()
    gather_a.start()
    for copy in yc_copies:
        copy.wait_recv()
    gather_c.start()
    for copy in zb_copies:
        copy.wait_recv()
    gather_b.start()
    gather_a.pass_on(1)
    gather_c.pass_on(1)
    gather_b.pass_on()
    gather_c.pass_on(2)
    gather_a.pass_on(2)
    gather_b.wait()
    gather_by.start()
    put_b(y)
    gather_c.pass_on(3)
    gather_a.pass_on(3)
    gather_c.wait()
    gather_cx.start()
    put_c(x)

    for copy in total_copies:
        copy.wait_recv()
    for first, width, out in ((0, 640, tv), (640, 640, ta), (1280, 4096, tl)):
        at = out.at[:, cols(width * c, width)]
        outs.append(load(totals.at[mine, pl.ds(first, width)], at))
        outs.append(send(totals.at[theirs, pl.ds(first, width)], at, core))

    gather_a.wait()
    put(all_a.at[:, :, :, pl.ds(0, 640)], pv.at[:, :, :, cols(640 * c, 640)])
    put(all_a.at[:, :, :, pl.ds(640, 640)], pa.at[:, :, :, cols(640 * c, 640)])
    gather_by.pass_on()
    put_b(yj(1))
    put_b(yj(3))
    gather_cx.pass_on()
    put_c(xj(1))
    put_c(xj(3))
    gather_by.wait()
    put_b(yj(2))
    gather_cx.wait()
    put_c(xj(2))

    for copy in outs:
        if copy.is_remote:
            copy.wait_recv()
        else:
            copy.wait()
    for wait_send in started:
        wait_send()


def whole_step(grads, states, step_counts):
    bf, f32 = jnp.bfloat16, jnp.float32
    vm = pltpu.VMEM
    scratch = [
        vm((8, 2, 16, 1280), bf), vm((4, 8, 16, 1024), bf), vm((4, 8, 2, 16, 512), bf),
        vm((8, 2, 16, 1280), bf), vm((4, 8, 16, 1024), bf), vm((4, 8, 2, 16, 512), bf),
        vm((8, 2, 16, 1280), f32), vm((4, 8, 16, 1024), f32), vm((4, 8, 2, 16, 512), f32),
        vm((4, 2, 16, 1280), f32), vm((4, 2, 16, 1280), f32),
        vm((4, 16, 1024), f32), vm((4, 16, 1024), f32), vm((8, 16, 1024), f32), vm((8, 16, 1024), f32),
        vm((4, 2, 16, 512), f32), vm((4, 2, 16, 512), f32), vm((8, 2, 16, 512), f32), vm((8, 2, 16, 512), f32),
        vm((2, 16, 1280), f32), vm((3, 16, 640), f32), vm((4, 16, 640), f32),
        vm((4, 8, 16, 256), f32), vm((4, 16, 256), f32), vm((4, 16, 256), f32),
        vm((8, 16, 256), f32), vm((8, 16, 256), f32), vm((8, 16, 256), f32), vm((7, 16, 256), f32),
        vm((8, 2, 16, 512), f32), vm((4, 2, 16, 512), f32), vm((4, 2, 16, 512), f32),
        vm((2, 16, 512), f32), vm((3, 16, 256), f32),
        vm((3, 2, 16, 640), f32), vm((3, 16, 256), f32), vm((3, 16, 256), f32), vm((16, 5376), f32),
        vm((8, 2, 16, 1280), bf), vm((4, 8, 16, 1024), bf), vm((4, 8, 2, 16, 512), bf),
        pltpu.SemaphoreType.DMA((N_SEMS,)),
    ]
    anywhere = pl.BlockSpec(memory_space=pl.ANY)
    return pl.pallas_call(
        step_kernel,
        out_shape=[
            jax.ShapeDtypeStruct((8, 2, 16, 1280), bf),
            jax.ShapeDtypeStruct((8, 2, 16, 1280), bf),
            jax.ShapeDtypeStruct((8, 2, 16, 8192), bf),
            jax.ShapeDtypeStruct((8, 1280), f32),
            jax.ShapeDtypeStruct((8, 1280), f32),
            jax.ShapeDtypeStruct((8, 8192), f32),
        ],
        in_specs=[anywhere] * 12 + [pl.BlockSpec(memory_space=pltpu.SMEM)],
        out_specs=[anywhere] * 6,
        scratch_shapes=scratch,
        compiler_params=pltpu.CompilerParams(
            collective_id=0, has_side_effects=True, vmem_limit_bytes=40 * 2**20
        ),
        name="sum_update_gather",
    )(*grads, *states, step_counts)


def state_kernel(tv, ta, tl, mv, ma, ml, nv, na, nl, sv, sa, sl, steps, *outs):
    for k, (t, m, n, s) in enumerate(((tv, mv, nv, sv), (ta, ma, na, sa), (tl, ml, nl, sl))):
        count = steps[k].astype(jnp.float32)
        new = adamw_update(t[...], m[...], n[...], s[...], count, 256.0)
        outs[k][...], outs[3 + k][...], outs[6 + k][...] = new


def update_states(totals, states, step_counts):
    whole = pl.BlockSpec(memory_space=pltpu.VMEM)
    return pl.pallas_call(
        state_kernel,
        out_shape=[jax.ShapeDtypeStruct(s.shape, s.dtype) for s in states],
        in_specs=[whole] * 12 + [pl.BlockSpec(memory_space=pltpu.SMEM)],
        out_specs=[whole] * 9,
        compiler_params=pltpu.CompilerParams(vmem_limit_bytes=16 * 2**20),
        name="update_states",
    )(*totals, *states, step_counts)


def per_device(*arguments):
    grads, states, step_counts = arguments[:3], arguments[3:12], arguments[12]
    grads = [g.reshape(8, 2, 16, g.shape[-1]) for g in grads]
    pv, pa, pm, *totals = whole_step(grads, states, step_counts)
    new_states = update_states(totals, states, step_counts)
    params = [p.reshape(256, p.shape[-1]) for p in (pv, pa, pm)]
    return (*params, *new_states)


def solution(mesh):
    grad, state = P("replica", "shard", None, None), P("shard", None)
    return jax.shard_map(
        per_device,
        mesh=mesh,
        in_specs=(grad,) * 3 + (state,) * 9 + (P(),),
        out_specs=(P(),) * 3 + (state,) * 9,
        check_vma=False,
    )
```

time: 673 us -> 102 us (0.15)
  waiting for transfers between devices: 547 us -> 0 us
  blocking collectives: 88.1 us -> 0 us
  Pallas kernels: 0 us -> 84.7 us
  between operations: 16.4 us -> 0.68 us
  other arithmetic: 13.7 us -> 0 us
  local copies, waits for them, and re-layouts: 7.88 us -> 16.2 us
    reduce_scatter x3 -> x0, waiting for transfers between devices: 385 us -> none  [the longest x1 150 us: per_device(): lax.psum_scatter(terms[2], 'shard', scatter_dimension=0, tiled=True)]
    psum x2 -> x0, waiting for transfers between devices: 154 us -> none  [per_device(): totals = lax.psum((shares[0], shares[1], shares[2]), 'replica')]
    all_gather x2 -> x0, blocking collectives: 88.1 us -> none  [the longest x1 49 us: per_device(): lax.all_gather(rounded[1], 'shard', axis=0, tiled=True)]
    pallas_call x0 -> x2, Pallas kernels: none -> 84.7 us  [the longest x1 83.1 us: whole_step(): pl.pallas_call(step_kernel, out_shape=[jax.ShapeDtypeStruct((8, 2, 16, 12...]
    convert_element_type x6 -> x0, other arithmetic: 13.7 us -> none  [the longest x3 8.8 us: per_device(): g.reshape(g.shape[2], g.shape[3]).astype(jnp.float32)]
    unnamed x27 -> x29, local copies, waits for them, and re-layouts: 7.29 us -> 16.2 us
    all_gather x1 -> x0, waiting for transfers between devices: 7.39 us -> none  [per_device(): lax.all_gather(rounded[2], 'shard', axis=0, tiled=True)]
  transfers between devices with their start and end apart: 6 -> 0, of which waited for: 6 -> 0; matrix products, arithmetic and copies ran while one was open for 1% -> 0% of each run, Pallas kernels for 0% -> 0%
where the time goes in v1:
time: 102 us
  Pallas kernels  84.7 us (83%)
  local copies, waits for them, and re-layouts  16.2 us (16%)
    pallas_call x1, Pallas kernels, whole_step(): pl.pallas_call(step_kernel, out_shape=[jax.ShapeDtypeStruct((8, 2, 16, 12...  83.1 us
    unnamed x29, local copies, waits for them, and re-layouts  16.2 us

profile of v1, /device:TPU:1, one launch (start us, length us, event | category | flops | bytes accessed | tf_op | source)
XLA Modules:
  0.0 101.6 jit_solution(15350431237947802706)
XLA Ops:
  0.6 0.0 copy-start
  0.7 2.2 %copy-done = bf16[1,1,256,8192]{3,2,1,0:T(8,128)(2,1)S(1)} copy-done((bf16[1,1,256,8192]{3,2,1,0:T(8,128)(2,1)S(1)}, bf16[1,1,256,8192]{3,2,1,0:T(8,128)(2,1)}, u32[]{:S(2)}) %copy-start) | copy-done | bytes 4194328
  2.8 0.0 copy-start.1
  2.8 0.9 copy-done.1
  3.8 0.0 copy-start.2
  3.8 0.9 copy-done.2
  4.7 0.0 copy-start.3
  4.7 0.9 copy-done.3
  5.7 0.0 copy-start.4
  5.7 1.1 %copy-done.4 = bf16[1,1,256,1280]{3,2,1,0:T(8,128)(2,1)S(1)} copy-done((bf16[1,1,256,1280]{3,2,1,0:T(8,128)(2,1)S(1)}, bf16[1,1,256,1280]{3,2,1,0:T(8,128)(2,1)}, u32[]{:S(2)}) %copy-start.4) | copy-done | bytes 655384
  6.8 0.0 copy-start.5
  6.8 1.1 %copy-done.5 = bf16[1,1,256,1280]{3,2,1,0:T(8,128)(2,1)S(1)} copy-done((bf16[1,1,256,1280]{3,2,1,0:T(8,128)(2,1)S(1)}, bf16[1,1,256,1280]{3,2,1,0:T(8,128)(2,1)}, u32[]{:S(2)}) %copy-start.5) | copy-done | bytes 655384
  7.9 0.0 copy-start.6
  7.9 0.8 copy-done.6
  8.6 0.0 copy-start.7
  8.6 0.8 copy-done.7
  9.4 0.0 copy-start.8
  9.4 0.8 copy-done.8
  10.2 0.0 copy-start.9
  10.2 0.8 copy-done.9
  11.0 0.0 copy-start.10
  11.0 0.8 copy-done.10
  11.8 0.0 copy-start.11
  11.8 0.8 copy-done.11
  12.5 0.0 copy-start.12
  12.5 0.7 copy-done.12
  13.2 83.1 %sum_update_gather.1 = (bf16[8,2,16,1280]{3,2,1,0:T(8,128)(2,1)S(1)}, bf16[8,2,16,1280]{3,2,1,0:T(8,128)(2,1)S(1)}, bf16[8,2,16,8192]{3,2,1,0:T(8,128)(2,1)S(1)}...) custom-call(bf16[8,2,16,1280]{3,2,1,0:T(8,128)(2,1)S(1)} %bitcast.10, ...), custom_call_target="tpu_custom_call" | custom-call | tf_op jit(solution)/shard_map/sum_update_gather/pallas_call | solution.py:539
  96.3 1.6 %update_states.1 = (f32[8,1280]{1,0:T(8,128)}, f32[8,1280]{1,0:T(8,128)}, f32[8,8192]{1,0:T(8,128)}, f32[8,1280]{1,0:T(8,128)}, f32[8,1280]{1,0:T(8,128)}, /*ind...) custom-call(f32[8,1280]{1,0:T(8,128)S(1)} %get-tuple-element.30.tv, ...), custom_call_target="tpu_custom_call" | custom-call | tf_op jit(solution)/shard_map/update_states/pallas_call | solution.py:568
  98.0 0.8 copy.28
  98.8 0.8 copy.29
  99.6 2.0 %copy.30 = bf16[256,8192]{1,0:T(8,128)(2,1)} copy(bf16[256,8192]{1,0:T(8,128)(2,1)S(1)} %bitcast.6) | data formatting | bytes 8388608
Async XLA Ops:
  0.6 2.2 %copy-start = (bf16[1,1,256,8192]{3,2,1,0:T(8,128)(2,1)S(1)}, bf16[1,1,256,8192]{3,2,1,0:T(8,128)(2,1)}, u32[]{:S(2)}) copy-start(bf16[1,1,256,8192]{3,2,1,0:T(8,128)(2,1)} %param.15) | copy-start | bytes 12582916
  2.8 0.9 copy-start.1
  3.8 0.9 copy-start.2
  4.7 0.9 copy-start.3
  5.7 1.1 %copy-start.4 = (bf16[1,1,256,1280]{3,2,1,0:T(8,128)(2,1)S(1)}, bf16[1,1,256,1280]{3,2,1,0:T(8,128)(2,1)}, u32[]{:S(2)}) copy-start(bf16[1,1,256,1280]{3,2,1,0:T(8,128)(2,1)} %param.13) | copy-start | bytes 1966084
  6.8 1.1 %copy-start.5 = (bf16[1,1,256,1280]{3,2,1,0:T(8,128)(2,1)S(1)}, bf16[1,1,256,1280]{3,2,1,0:T(8,128)(2,1)}, u32[]{:S(2)}) copy-start(bf16[1,1,256,1280]{3,2,1,0:T(8,128)(2,1)} %param.14) | copy-start | bytes 1966084
  7.9 0.8 copy-start.6
  8.6 0.8 copy-start.7
  9.4 0.8 copy-start.8
  10.2 0.8 copy-start.9
  11.0 0.8 copy-start.10
  11.8 0.8 copy-start.11
  12.5 0.7 copy-start.12

commit v2 on v0

v2 whole, which is shorter than its diff:
```python
import math

import jax
import jax.numpy as jnp
from jax import lax
from jax.experimental import pallas as pl
from jax.experimental.pallas import tpu as pltpu
from jax.sharding import PartitionSpec as P

BETA_ONE = 0.9
BETA_TWO = 0.95
EPSILON = 1e-08
WEIGHT_DECAY = 0.1
LEARN_RATE = 0.002
MESH = pl.DeviceIdType.MESH
N_SEMS = 640


def adamw_update(grad_sum, master, moment, second, steps, devices_all):
    grad = grad_sum * (1.0 / devices_all)
    moment_new = BETA_ONE * moment + (1.0 - BETA_ONE) * grad
    second_new = BETA_TWO * second + (1.0 - BETA_TWO) * grad * grad
    t = jnp.full(grad_sum.shape, steps, jnp.float32)
    first_fix = 1.0 - jnp.exp(t * math.log(BETA_ONE))
    second_fix = 1.0 - jnp.exp(t * math.log(BETA_TWO))
    update = (
        moment_new / first_fix / (jnp.sqrt(second_new / second_fix) + EPSILON)
        + WEIGHT_DECAY * master
    )
    master_new = master - LEARN_RATE * update
    return master_new, moment_new, second_new


def coordinates():
    s, r = lax.axis_index("shard"), lax.axis_index("replica")
    z, yh, c = lax.div(s, 4), lax.rem(lax.div(s, 2), 2), lax.rem(s, 2)
    yl, x = lax.div(r, 4), lax.rem(r, 4)
    return x, yh, yl, z, c


def device(x, y, z, c):
    return (z * 4 + lax.div(y, 2) * 2 + c, lax.rem(y, 2) * 4 + x)


def cols(start, size):
    return pl.ds(pl.multiple_of(start, 128), size)


def step_kernel(
    gv, ga, gl, mv, ma, ml, nv, na, nl, sv, sa, sl, steps,
    pv, pa, pm, mv_out, ma_out, ml_out, nv_out, na_out, nl_out, sv_out, sa_out, sl_out,
    own_v, own_a, own_m, got_v, got_a, got_b, got_c, sum_a, sum_b, sum_c, rm_a, lm_a,
    b_r2, b_l2, b_from_l, b_from_r, c_r2, c_l2, c_from_l, c_from_r,
    a1, a2_got, a3_all, rm_b, lm_b, rm_c, lm_c, b2, b3_got, c2, c3_got,
    st_a, st_b, st_c, state_v, state_a, state_m, totals, total_v, total_a, total_m,
    all_a, new_b, new_c, counts, sems,
):
    x, yh, yl, z, c = coordinates()
    y = yh * 2 + yl
    other = 1 - c
    f32, bf = jnp.float32, jnp.bfloat16

    def xj(j):
        return lax.rem(x + j, 4)

    def yj(j):
        return lax.rem(y + j, 4)

    def zj(j):
        return lax.rem(z + j, 8)

    core = device(x, y, z, other)
    right_x, left_x = device(xj(1), y, z, c), device(xj(3), y, z, c)
    right_y, left_y = device(x, yj(1), z, c), device(x, yj(3), z, c)
    right_z, left_z = device(x, y, zj(1), c), device(x, y, zj(7), c)
    y_twin = yh * 2 + (1 - yl)

    used = [0]
    started = []

    def sem():
        used[0] += 1
        return sems.at[used[0] - 1]

    def send(src, dst, to):
        copy = pltpu.make_async_remote_copy(
            src_ref=src, dst_ref=dst, send_sem=sem(), recv_sem=sem(),
            device_id=to, device_id_type=MESH,
        )
        copy.start()
        started.append(copy.wait_send)
        return copy

    def load(src, dst):
        copy = pltpu.make_async_copy(src, dst, sem())
        copy.start()
        return copy

    barrier = pltpu.get_barrier_semaphore()
    peers = [core]
    peers += [device(x, y, zj(k), c) for k in (2, 6, 1, 7)]
    peers += [device(xj(k), y, z, c) for k in range(1, 4)]
    peers += [device(x, yj(k), z, c) for k in range(1, 4)]
    peers += [device(xj(k), y_twin, z, c) for k in range(1, 4)]
    for peer in peers:
        pl.semaphore_signal(barrier, inc=1, device_id=peer, device_id_type=MESH)
    own_copies = {
        "m": load(gl.at[:, :, :, cols(4096 * c, 4096)], own_m),
        "v": load(gv.at[:, :, :, cols(640 * c, 640)], own_v),
        "a": load(ga.at[:, :, :, cols(640 * c, 640)], own_a),
    }
    pl.semaphore_wait(barrier, len(peers))

    order = [("b", 2), ("c", 2), ("b", 1), ("c", 1), ("b", 3), ("c", 3), ("v", 0), ("a", 0), ("b", 0), ("c", 0)]
    core_copies, taken = {}, set()

    def core_send():
        if len(core_copies) == len(order):
            return
        part, j = order[len(core_copies)]
        if part == "b":
            yy = yj(j)
            src = gl.at[:, lax.div(yy, 2), :, cols(4096 * other + lax.rem(yy, 2) * 1024, 1024)]
            dst = got_b.at[j]
        elif part == "c":
            src = gl.at[:, :, :, cols(4096 * other + 2048 + xj(j) * 512, 512)]
            dst = got_c.at[j]
        else:
            src = (gv if part == "v" else ga).at[:, :, :, cols(640 * other, 640)]
            dst = got_v if part == "v" else got_a
        core_copies[part, j] = send(src, dst, core)

    def take(own, part, j):
        if own not in taken:
            own_copies[own].wait()
            taken.add(own)
        if (part, j) not in taken:
            core_copies[part, j].wait_recv()
            core_send()
            taken.add((part, j))

    place = {4: 0, 3: 1, 5: 2, 2: 3, 6: 4, 1: 5, 7: 6, 0: 7}

    def z_at(p):
        return zj(4 + lax.div(p + 1, 2) * (2 * lax.rem(p + 1, 2) - 1))

    def chip_sum_b(j, first=0, n=8):
        take("m", "b", j)
        yy = yj(j)
        high, low = lax.div(yy, 2), lax.rem(yy, 2) * 1024

        def body(p, _):
            zz = z_at(p)
            for h in (0, 1):
                here = own_m[zz, high, :, cols(low + h * 512, 512)].astype(f32)
                sum_b[j, p, h] = here + got_b[j, zz, :, pl.ds(h * 512, 512)].astype(f32)
            return 0

        lax.fori_loop(first, first + n, body, 0)

    def chip_sum_c(j, first=0, n=8):
        take("m", "c", j)
        at = cols(2048 + xj(j) * 512, 512)

        def body(p, _):
            zz = z_at(p)
            for h in (0, 1):
                sum_c[j, p, h] = own_m[zz, h, :, at].astype(f32) + got_c[j, zz, h].astype(f32)
            return 0

        lax.fori_loop(first, first + n, body, 0)

    def chip_sum_a(j):
        zz = zj(j)
        sum_a[j, :, :, 0:640] = own_v[zz].astype(f32) + got_v[zz].astype(f32)
        sum_a[j, :, :, 640:1280] = own_a[zz].astype(f32) + got_a[zz].astype(f32)

    class Ring4:
        def __init__(self, piece, r2, l2, from_l, from_r, right, left):
            self.piece, self.r2, self.l2, self.from_l, self.from_r = piece, r2, l2, from_l, from_r
            self.right, self.left = right, left

        def far(self):
            self.c_r2 = send(self.piece(2, 0), self.r2, self.right)
            self.c_l2 = send(self.piece(2, 1), self.l2, self.left)

        def near_right(self):
            self.c_r1 = send(self.piece(1, 1), self.from_l(1), self.right)

        def near_left(self):
            self.c_l0 = send(self.piece(3, 0), self.from_r(0), self.left)

        def pass_on(self):
            self.c_r2.wait_recv()
            at = self.piece(1, 0)
            at[...] = at[...] + self.r2[...]
            self.c_r0 = send(at, self.from_l(0), self.right)
            self.c_l2.wait_recv()
            at = self.piece(3, 1)
            at[...] = at[...] + self.l2[...]
            self.c_l1 = send(at, self.from_r(1), self.left)

        def end(self):
            for copy in (self.c_r1, self.c_l0, self.c_r0, self.c_l1):
                copy.wait_recv()
            for h in (0, 1):
                at = self.piece(0, h)
                at[...] = at[...] + self.from_l(h)[...] + self.from_r(h)[...]

    class Ring8:
        def __init__(self, at, rm, lm):
            self.at, self.rm, self.lm = at, rm, lm
            self.r, self.l = {}, {}

        def send_right(self, m, h):
            self.r[m - 1, h] = send(self.at(m, h), self.rm(m - 1, h), right_z)

        def send_left(self, m, h):
            self.l[m - 1, h] = send(self.at((8 - m) % 8, h), self.lm(m - 1, h), left_z)

        def first(self):
            self.send_right(4, 0)
            self.send_left(4, 1)

        def second(self):
            self.send_right(3, 1)
            self.send_left(3, 0)

        def step(self, m, h):
            self.r[m, h].wait_recv()
            at = self.at(m, h)
            at[...] = at[...] + self.rm(m, h)[...]
            self.send_right(m, h)
            self.l[m, 1 - h].wait_recv()
            at = self.at(8 - m, 1 - h)
            at[...] = at[...] + self.lm(m, 1 - h)[...]
            self.send_left(m, 1 - h)

        def end(self, out):
            for h in (0, 1):
                self.r[0, h].wait_recv()
                self.l[0, h].wait_recv()
                out(h)[...] = self.at(0, h)[...] + self.rm(0, h)[...] + self.lm(0, h)[...]

    def ring4(total, r2, l2, from_l, from_r, right, left, first, n):
        at = pl.ds(first, n)
        return Ring4(
            lambda j, h: total.at[j, at, h], r2.at[at], l2.at[at],
            lambda h: from_l.at[at, h], lambda h: from_r.at[at, h], right, left,
        )

    def ring8(total, rm, lm):
        return Ring8(lambda m, h: total.at[0, place[m], h], lambda m, h: rm.at[m, h], lambda m, h: lm.at[m, h])

    def columns_a(ref):
        return lambda m, h: ref.at[m, :, :, pl.ds(640 * h, 640)]

    groups = ((0, 3), (3, 2), (5, 2), (7, 1))
    rb = [ring4(sum_b, b_r2, b_l2, b_from_l, b_from_r, right_y, left_y, *g) for g in groups]
    rc = [ring4(sum_c, c_r2, c_l2, c_from_l, c_from_r, right_x, left_x, *g) for g in groups]
    ring_a = Ring8(columns_a(sum_a), columns_a(rm_a), columns_a(lm_a))
    ring_b, ring_c = ring8(sum_b, rm_b, lm_b), ring8(sum_c, rm_c, lm_c)

    for _ in range(4):
        core_send()
    chip_sum_b(2, 0, 3)
    rb[0].far()
    chip_sum_c(2, 0, 3)
    rc[0].far()
    chip_sum_b(2, 3, 5)
    rb[1].far()
    chip_sum_c(2, 3, 5)
    rc[1].far()
    chip_sum_b(1)
    rb[0].near_right()
    chip_sum_c(1)
    rc[0].near_right()
    chip_sum_b(3)
    rb[0].near_left()
    chip_sum_c(3)
    rc[0].near_left()
    for ring in (rb[1], rc[1]):
        ring.near_right()
        ring.near_left()
    take("v", "v", 0)
    take("a", "a", 0)
    chip_sum_a(4)
    ring_a.first()
    rb[0].pass_on()
    rc[0].pass_on()
    chip_sum_a(3)
    chip_sum_a(5)
    ring_a.second()

    def first_sends(ring):
        ring.far()
        ring.near_right()
        ring.near_left()

    first_sends(rb[2])
    first_sends(rc[2])
    chip_sum_a(2)
    chip_sum_a(6)
    chip_sum_b(0)
    chip_sum_c(0)
    ring_a.step(3, 0)
    rb[1].pass_on()
    rc[1].pass_on()
    first_sends(rb[3])
    first_sends(rc[3])
    rb[0].end()
    ring_b.first()
    ring_b.second()
    rc[0].end()
    ring_c.first()
    ring_c.second()
    chip_sum_a(1)
    chip_sum_a(7)
    chip_sum_a(0)
    ring_a.step(2, 1)

    col_a, col_b, col_c = yl * 640, yl * 1024 + x * 256, 2048 + x * 512 + yl * 256
    mine, theirs = pl.ds(pl.multiple_of(c * 8, 8), 8), pl.ds(pl.multiple_of(other * 8, 8), 8)
    inputs = ((mv, ma, ml), (nv, na, nl), (sv, sa, sl))

    def state_pieces(half):
        pairs = []
        for k, (v, a, m) in enumerate(inputs):
            pairs.append((v.at[:, cols(640 * half, 640)], st_a.at[k, 0, mine]))
            pairs.append((a.at[:, cols(640 * half, 640)], st_a.at[k, 1, mine]))
            pairs.append((m.at[:, cols(4096 * half + col_b, 256)], st_b.at[k, mine]))
            pairs.append((m.at[:, cols(4096 * half + col_c, 256)], st_c.at[k, mine]))
        return pairs

    state_copies = [load(src, dst) for src, dst in state_pieces(c)] + [load(steps, counts)]
    state_sends = [send(src, dst, core) for src, dst in state_pieces(other)]
    for k, (v, a, m) in enumerate(inputs):
        state_copies += [load(v, state_v.at[k]), load(a, state_a.at[k]), load(m, state_m.at[k])]

    rb[2].pass_on()
    rc[2].pass_on()
    ring_a.step(2, 0)
    rb[1].end()
    ring_b.step(3, 0)
    ring_b.step(2, 1)
    rc[1].end()
    ring_c.step(3, 0)
    ring_c.step(2, 1)
    ring_a.step(1, 1)
    rb[3].pass_on()
    rc[3].pass_on()
    rb[2].end()
    rc[2].end()
    ring_b.step(1, 1)
    ring_c.step(1, 1)
    ring_b.step(2, 0)
    ring_c.step(2, 0)
    ring_a.step(1, 0)
    rb[3].end()
    rc[3].end()
    ring_b.step(1, 0)
    ring_c.step(1, 0)

    ring_a.end(lambda h: a1.at[:, :, pl.ds(640 * h, 640)])
    a2_copies = []
    for k in range(1, 4):
        yy = yj(k)
        src = a1.at[lax.div(yy, 2), :, cols(lax.rem(yy, 2) * 640, 640)]
        a2_copies.append(send(src, a2_got.at[k - 1], device(x, yy, z, c)))

    def owned(ref, i):
        return ref.at[lax.div(i, 2), :, cols(lax.rem(i, 2) * 256, 256)]

    ring_b.end(lambda h: b2.at[h])
    b3_copies = [send(owned(b2, xj(k)), b3_got.at[k - 1], device(xj(k), y, z, c)) for k in (2, 1, 3)]
    ring_c.end(lambda h: c2.at[h])
    c3_copies = [send(owned(c2, yj(k)), c3_got.at[k - 1], device(x, yj(k), z, c)) for k in (2, 1, 3)]
    for copy in a2_copies:
        copy.wait_recv()
    a3_all[x] = a1[yh, :, cols(yl * 640, 640)] + a2_got[0] + a2_got[1] + a2_got[2]
    a3_copies = [send(a3_all.at[x], a3_all.at[x], device(xj(k), y, z, c)) for k in range(1, 4)]

    for copy in state_copies:
        copy.wait()
    for copy in state_sends:
        copy.wait_recv()
    t_vision, t_audio, t_lm = (counts[k].astype(f32) for k in range(3))

    def at_b(yy, zz, h=None):
        first = 4096 * c + lax.rem(yy, 2) * 1024
        at = cols(first, 1024) if h is None else cols(first + 512 * h, 512)
        return pm.at[zz, lax.div(yy, 2), :, at]

    def at_c(xx, zz, h=None):
        return pm.at[zz, slice(None) if h is None else h, :, cols(4096 * c + 2048 + xx * 512, 512)]

    def update_owned(partial, i, got, copies, first, state, new):
        for copy in copies:
            copy.wait_recv()
        total = owned(partial, i)[...] + got[0] + got[1] + got[2]
        totals[:, cols(1280 + first, 256)] = total
        new[...] = adamw_update(total, state[0], state[1], state[2], t_lm, 256.0)[0].astype(bf)

    update_owned(b2, x, b3_got, b3_copies, col_b, st_b, new_b)
    at = pm.at[z, yh, :, cols(4096 * c + col_b, 256)]
    own_b = load(new_b, at)
    xb_copies = [send(new_b, at, device(xj(k), y, z, c)) for k in (2, 1, 3)]
    update_owned(c2, y, c3_got, c3_copies, col_c, st_c, new_c)
    at = pm.at[z, yh, :, cols(4096 * c + col_c, 256)]
    own_c = load(new_c, at)
    yc_copies = [send(new_c, at, device(x, yj(k), z, c)) for k in (2, 1, 3)]
    for copy in a3_copies:
        copy.wait_recv()
    total = (a3_all[0] + a3_all[1]) + (a3_all[2] + a3_all[3])
    totals[:, cols(yl * 640, 640)] = total
    t_a = jnp.where(yl == 0, t_vision, t_audio)
    updated = adamw_update(total, st_a[0, yl], st_a[1, yl], st_a[2, yl], t_a, 256.0)[0]
    all_a[z, yh, :, cols(yl * 640, 640)] = updated.astype(bf)
    at = all_a.at[z, yh, :, cols(yl * 640, 640)]
    ya_copies = [send(at, at, device(x, yj(k), z, c)) for k in (2, 1, 3)]

    class Relay4:
        def __init__(self, at, right, left, me, by_right):
            self.at, self.me, self.right, self.left, self.by_right = at, me, right, left, by_right

        def start(self):
            own = self.at(self.me)
            self.r = send(own, own, self.right)
            self.l = send(own, own, self.left)

        def pass_on(self):
            if self.by_right:
                self.r.wait_recv()
                at = self.at(lax.rem(self.me + 3, 4))
                self.far = send(at, at, self.right)
            else:
                self.l.wait_recv()
                at = self.at(lax.rem(self.me + 1, 4))
                self.far = send(at, at, self.left)

        def wait_near(self):
            (self.l if self.by_right else self.r).wait_recv()

    class Gather8:
        def __init__(self, at):
            self.at = at

        def start(self):
            own = self.at(z, None)
            self.r = send(own, own, right_z)
            self.l = send(own, own, left_z)

        def pass_on(self, k):
            self.r.wait_recv()
            at = self.at(zj(8 - k), 0 if k == 3 else None)
            self.r = send(at, at, right_z)
            self.l.wait_recv()
            at = self.at(zj(k), 1 if k == 3 else None)
            self.l = send(at, at, left_z)

        def wait(self):
            self.r.wait_recv()
            self.l.wait_recv()

    def at_a8(zz, h):
        if h is None:
            return all_a.at[zz]
        return all_a.at[zz, :, :, pl.ds(640 * h, 640)]

    class Block8:
        def __init__(self, at):
            self.at = at

        def start(self):
            own = self.at(z, None)
            self.r1, self.l1 = send(own, own, right_z), send(own, own, left_z)
            self.r2 = send(own, own, device(x, y, zj(2), c))
            self.l2 = send(own, own, device(x, y, zj(6), c))

        def near(self):
            self.r1.wait_recv()
            self.l1.wait_recv()

        def pass_on(self):
            self.r2.wait_recv()
            at, part = self.at(zj(6), None), self.at(zj(6), 0)
            self.r3 = send(at, at, right_z)
            self.r4 = send(part, part, device(x, y, zj(2), c))
            self.l2.wait_recv()
            at, part = self.at(zj(2), None), self.at(zj(2), 1)
            self.l3 = send(at, at, left_z)
            self.l4 = send(part, part, device(x, y, zj(6), c))

        def third(self):
            self.r3.wait_recv()
            self.l3.wait_recv()

        def fourth(self):
            self.r4.wait_recv()
            self.l4.wait_recv()

    outs = []

    def put(at):
        outs.append(send(at, at, core))

    def put_a(ref, first):
        src, dst = all_a.at[:, :, :, pl.ds(first, 640)], ref.at[:, :, :, cols(640 * c, 640)]
        outs.append(load(src, dst))
        outs.append(send(src, dst, core))

    def put_b(yy):
        put(pm.at[:, lax.div(yy, 2), :, cols(4096 * c + lax.rem(yy, 2) * 1024, 1024)])

    gather_a = Gather8(at_a8)
    gather_b, gather_c = Block8(lambda zz, h: at_b(y, zz, h)), Block8(lambda zz, h: at_c(x, zz, h))
    by = [Relay4(lambda i, m=m: at_b(i, zj(m)), right_y, left_y, y, m < 4) for m in range(8)]
    cx = [Relay4(lambda i, m=m: at_c(i, zj(m)), right_x, left_x, x, m < 4) for m in range(8)]

    def relays_start(*ms):
        for relays in (by, cx):
            for m in ms:
                relays[m].start()

    def relays_pass(*ms):
        for relays in (by, cx):
            for m in ms:
                relays[m].pass_on()

    own_b.wait()
    for copy in xb_copies:
        copy.wait_recv()
    by[0].start()
    gather_b.start()
    own_c.wait()
    for copy in yc_copies:
        copy.wait_recv()
    cx[0].start()
    gather_c.start()
    for copy in ya_copies:
        copy.wait_recv()
    gather_a.start()
    gather_b.near()
    gather_c.near()
    relays_start(1, 7)
    gather_b.pass_on()
    gather_c.pass_on()
    relays_start(2, 6)
    relays_pass(0)
    gather_a.pass_on(1)
    at_ta, at_tb, at_tc = (totals.at[:, cols(o, w)] for o, w in ((col_a, 640), (1280 + col_b, 256), (1280 + col_c, 256)))
    total_copies = [send(at_ta, at_ta, device(x, y_twin, z, c))]
    for k in range(4):
        for yy in (y, y_twin):
            if k or yy is not y:
                total_copies.append(send(at_tb, at_tb, device(xj(k), yy, z, c)))
                total_copies.append(send(at_tc, at_tc, device(xj(k), yy, z, c)))
    relays_pass(1, 7)
    gather_b.third()
    gather_c.third()
    relays_start(3, 5)
    gather_b.fourth()
    gather_c.fourth()
    relays_start(4)
    put_b(y)
    put(at_c(x, slice(None)))
    relays_pass(2, 6)
    gather_a.pass_on(2)
    relays_pass(3, 5)
    relays_pass(4)
    gather_a.pass_on(3)

    for copy in total_copies:
        copy.wait_recv()
    row_copies = []
    for first, width, out in ((0, 640, total_v), (640, 640, total_a), (1280, 4096, total_m)):
        at = out.at[:, cols(width * c, width)]
        row_copies.append(load(totals.at[mine, pl.ds(first, width)], at))
        row_copies.append(send(totals.at[theirs, pl.ds(first, width)], at, core))
    for relay in by + cx:
        relay.wait_near()
    put_b(yj(1))
    put_b(yj(3))
    put(at_c(xj(1), slice(None)))
    put(at_c(xj(3), slice(None)))
    for copy in row_copies:
        if copy.is_remote:
            copy.wait_recv()
        else:
            copy.wait()

    def update_state(total, state, t, at):
        new = adamw_update(total[:, at], state[0, :, at], state[1, :, at], state[2, :, at], t, 256.0)
        for k in range(3):
            state[k, :, at] = new[k]

    update_state(total_v, state_v, t_vision, pl.ds(0, 1280))
    update_state(total_a, state_a, t_audio, pl.ds(0, 1280))

    def update_columns(i, _):
        update_state(total_m, state_m, t_lm, cols(i * 1024, 1024))
        return 0

    lax.fori_loop(0, 8, update_columns, 0)
    new_states = ((mv_out, ma_out, ml_out), (nv_out, na_out, nl_out), (sv_out, sa_out, sl_out))
    for k, (v, a, m) in enumerate(new_states):
        outs += [load(state_v.at[k], v), load(state_a.at[k], a), load(state_m.at[k], m)]
    for m in (0, 1, 7, 2, 6, 3, 5, 4):
        by[m].far.wait_recv()
        put(at_b(yj(2), zj(m)))
        cx[m].far.wait_recv()
        put(at_c(xj(2), zj(m)))
    gather_a.wait()
    put_a(pv, 0)
    put_a(pa, 640)
    for copy in outs:
        if copy.is_remote:
            copy.wait_recv()
        else:
            copy.wait()
    for wait_send in started:
        wait_send()


def whole_step(grads, states, step_counts):
    bf, f32 = jnp.bfloat16, jnp.float32
    vm = pltpu.VMEM
    scratch = [
        vm((8, 2, 16, 640), bf), vm((8, 2, 16, 640), bf), vm((8, 2, 16, 4096), bf),
        vm((8, 2, 16, 640), bf), vm((8, 2, 16, 640), bf), vm((4, 8, 16, 1024), bf), vm((4, 8, 2, 16, 512), bf),
        vm((8, 2, 16, 1280), f32), vm((4, 8, 2, 16, 512), f32), vm((4, 8, 2, 16, 512), f32),
        vm((4, 2, 16, 1280), f32), vm((4, 2, 16, 1280), f32),
        *[vm((8, 16, 512), f32), vm((8, 16, 512), f32), vm((8, 2, 16, 512), f32), vm((8, 2, 16, 512), f32)] * 2,
        vm((2, 16, 1280), f32), vm((3, 16, 640), f32), vm((4, 16, 640), f32),
        *[vm((4, 2, 16, 512), f32)] * 4,
        *[vm((2, 16, 512), f32), vm((3, 16, 256), f32)] * 2,
        vm((3, 2, 16, 640), f32), vm((3, 16, 256), f32), vm((3, 16, 256), f32),
        vm((3, 8, 1280), f32), vm((3, 8, 1280), f32), vm((3, 8, 8192), f32),
        vm((16, 5376), f32), vm((8, 1280), f32), vm((8, 1280), f32), vm((8, 8192), f32),
        vm((8, 2, 16, 1280), bf), vm((16, 256), bf), vm((16, 256), bf),
        pltpu.SMEM((3,), jnp.int32),
        pltpu.SemaphoreType.DMA((N_SEMS,)),
    ]
    anywhere, hbm = pl.BlockSpec(memory_space=pl.ANY), pl.BlockSpec(memory_space=pltpu.HBM)
    shapes = [((8, 2, 16, g.shape[-1]), bf) for g in grads] + [(s.shape, f32) for s in states]
    return pl.pallas_call(
        step_kernel,
        out_shape=[pltpu.VMEM(*s) for s in shapes],
        in_specs=[hbm] * 13,
        out_specs=[anywhere] * 12,
        scratch_shapes=scratch,
        compiler_params=pltpu.CompilerParams(
            collective_id=0, has_side_effects=True, vmem_limit_bytes=32 * 2**20
        ),
        name="sum_update_gather",
    )(*[pltpu.with_memory_space_constraint(a, pltpu.HBM) for a in (*grads, *states, step_counts)])


def copy_kernel(*refs):
    n = len(refs) // 2
    sems = refs[-1]
    copies = [pltpu.make_async_copy(refs[k], refs[n + k], sems.at[k]) for k in range(n)]
    for copy in copies:
        copy.start()
    for copy in copies:
        copy.wait()


def copy_out(arrays):
    n = len(arrays)
    anywhere = pl.BlockSpec(memory_space=pl.ANY)
    return pl.pallas_call(
        copy_kernel,
        out_shape=[pltpu.HBM(a.shape, a.dtype) for a in arrays],
        in_specs=[anywhere] * n,
        out_specs=[anywhere] * n,
        scratch_shapes=[pltpu.SemaphoreType.DMA((n,))],
        compiler_params=pltpu.CompilerParams(vmem_limit_bytes=2**20),
        name="copy_out",
    )(*[pltpu.with_memory_space_constraint(a, pltpu.VMEM) for a in arrays])


def per_device(*arguments):
    grads, states, step_counts = arguments[:3], arguments[3:12], arguments[12]
    grads = [g.reshape(8, 2, 16, g.shape[-1]) for g in grads]
    results = copy_out(whole_step(grads, states, step_counts))
    return (*[p.reshape(256, p.shape[-1]) for p in results[:3]], *results[3:])


def solution(mesh):
    grad, state = P("replica", "shard", None, None), P("shard", None)
    return jax.shard_map(
        per_device,
        mesh=mesh,
        in_specs=(grad,) * 3 + (state,) * 9 + (P(),),
        out_specs=(P(),) * 3 + (state,) * 9,
        check_vma=False,
    )
```

time: 673 us -> 81.8 us (0.12)
  waiting for transfers between devices: 547 us -> 0 us
  blocking collectives: 88.1 us -> 0 us
  Pallas kernels: 0 us -> 81 us
  between operations: 16.4 us -> 0.66 us
  other arithmetic: 13.7 us -> 0 us
  local copies, waits for them, and re-layouts: 7.88 us -> 0 us
    reduce_scatter x3 -> x0, waiting for transfers between devices: 385 us -> none  [the longest x1 150 us: per_device(): lax.psum_scatter(terms[2], 'shard', scatter_dimension=0, tiled=True)]
    psum x2 -> x0, waiting for transfers between devices: 154 us -> none  [per_device(): totals = lax.psum((shares[0], shares[1], shares[2]), 'replica')]
    all_gather x2 -> x0, blocking collectives: 88.1 us -> none  [the longest x1 49 us: per_device(): lax.all_gather(rounded[1], 'shard', axis=0, tiled=True)]
    pallas_call x0 -> x2, Pallas kernels: none -> 81 us  [the longest x1 78.1 us: whole_step(): pl.pallas_call(step_kernel, out_shape=[pltpu.VMEM(*s) for s in shapes], i...]
    convert_element_type x6 -> x0, other arithmetic: 13.7 us -> none  [the longest x3 8.8 us: per_device(): g.reshape(g.shape[2], g.shape[3]).astype(jnp.float32)]
    all_gather x1 -> x0, waiting for transfers between devices: 7.39 us -> none  [per_device(): lax.all_gather(rounded[2], 'shard', axis=0, tiled=True)]
    unnamed x27 -> x0, local copies, waits for them, and re-layouts: 7.29 us -> none
  transfers between devices with their start and end apart: 6 -> 0, of which waited for: 6 -> 0; matrix products, arithmetic and copies ran while one was open for 1% -> 0% of each run, Pallas kernels for 0% -> 0%
where the time goes in v2:
time: 81.8 us; the launch traced here: 81.7 us
  Pallas kernels  81 us (99%)
    pallas_call x1, Pallas kernels, whole_step(): pl.pallas_call(step_kernel, out_shape=[pltpu.VMEM(*s) for s in shapes], i...  78.1 us
    pallas_call x1, Pallas kernels, copy_out(): pl.pallas_call(copy_kernel, out_shape=[pltpu.HBM(a.shape, a.dtype) for a...  2.86 us

profile of v2, /device:TPU:1, one launch (start us, length us, event | category | flops | bytes accessed | tf_op | source)
XLA Modules:
  0.0 81.7 jit_solution(16253364019415458613)
XLA Ops:
  0.6 78.1 %sum_update_gather.1 = (bf16[8,2,16,1280]{3,2,1,0:T(8,128)(2,1)S(1)}, bf16[8,2,16,1280]{3,2,1,0:T(8,128)(2,1)S(1)}, bf16[8,2,16,8192]{3,2,1,0:T(8,128)(2,1)S(1)}...) custom-call(bf16[8,2,16,1280]{3,2,1,0:T(8,128)(2,1)} %bitcast.7, ...), custom_call_target="tpu_custom_call" | custom-call | tf_op jit(solution)/shard_map/sum_update_gather/pallas_call | solution.py:646
  78.8 2.9 %copy_out.1 = (bf16[8,2,16,1280]{3,2,1,0:T(8,128)(2,1)}, bf16[8,2,16,1280]{3,2,1,0:T(8,128)(2,1)}, bf16[8,2,16,8192]{3,2,1,0:T(8,128)(2,1)}, f32[8,1280]{1,0:T(8...) custom-call(bf16[8,2,16,1280]{3,2,1,0:T(8,128)(2,1)S(1)} %get-tuple-, ...), custom_call_target="tpu_custom_call" | custom-call | tf_op jit(solution)/shard_map/copy_out/pallas_call | solution.py:672

commit v3 on v2

--- a/solution.py
+++ b/solution.py
@@ -13,7 +13,7 @@
 WEIGHT_DECAY = 0.1
 LEARN_RATE = 0.002
 MESH = pl.DeviceIdType.MESH
-N_SEMS = 640
+N_SEMS = 800
 
 
 def adamw_update(grad_sum, master, moment, second, steps, devices_all):
@@ -91,6 +91,15 @@
         started.append(copy.wait_send)
         return copy
 
+    def seen():
+        past = started[:]
+        started.clear()
+        return past
+
+    def drain(past):
+        for wait in past:
+            wait()
+
     def load(src, dst):
         copy = pltpu.make_async_copy(src, dst, sem())
         copy.start()
@@ -98,7 +107,7 @@
 
     barrier = pltpu.get_barrier_semaphore()
     peers = [core]
-    peers += [device(x, y, zj(k), c) for k in (2, 6, 1, 7)]
+    peers += [device(x, y, zj(k), c) for k in (4, 3, 5, 2, 6, 1, 7)]
     peers += [device(xj(k), y, z, c) for k in range(1, 4)]
     peers += [device(x, yj(k), z, c) for k in range(1, 4)]
     peers += [device(xj(k), y_twin, z, c) for k in range(1, 4)]
@@ -111,41 +120,44 @@
     }
     pl.semaphore_wait(barrier, len(peers))
 
-    order = [("b", 2), ("c", 2), ("b", 1), ("c", 1), ("b", 3), ("c", 3), ("v", 0), ("a", 0), ("b", 0), ("c", 0)]
+    order = [("a", 4), ("b", 2, 0, 3), ("c", 2, 0, 3), ("a", 3), ("a", 5), ("b", 2, 3, 5), ("c", 2, 3, 5), ("b", 1), ("c", 1),
+             ("b", 3), ("c", 3), ("a", 2), ("a", 6), ("b", 0), ("c", 0), ("a", 1), ("a", 7), ("a", 0)]
     core_copies, taken = {}, set()
+
+    place = {4: 0, 3: 1, 5: 2, 2: 3, 6: 4, 1: 5, 7: 6, 0: 7}
+
+    def z_at(p):
+        return zj(4 + lax.div(p + 1, 2) * (2 * lax.rem(p + 1, 2) - 1))
 
     def core_send():
         if len(core_copies) == len(order):
             return
-        part, j = order[len(core_copies)]
+        part, j, *blocks = piece = order[len(core_copies)]
+        where = [z_at(jnp.int32(p)) for p in range(blocks[0], sum(blocks))] if blocks else [slice(None)]
         if part == "b":
             yy = yj(j)
-            src = gl.at[:, lax.div(yy, 2), :, cols(4096 * other + lax.rem(yy, 2) * 1024, 1024)]
-            dst = got_b.at[j]
+            at = cols(4096 * other + lax.rem(yy, 2) * 1024, 1024)
+            pairs = [(gl.at[zz, lax.div(yy, 2), :, at], got_b.at[j, zz]) for zz in where]
         elif part == "c":
-            src = gl.at[:, :, :, cols(4096 * other + 2048 + xj(j) * 512, 512)]
-            dst = got_c.at[j]
+            at = cols(4096 * other + 2048 + xj(j) * 512, 512)
+            pairs = [(gl.at[zz, :, :, at], got_c.at[j, zz]) for zz in where]
         else:
-            src = (gv if part == "v" else ga).at[:, :, :, cols(640 * other, 640)]
-            dst = got_v if part == "v" else got_a
-        core_copies[part, j] = send(src, dst, core)
-
-    def take(own, part, j):
-        if own not in taken:
-            own_copies[own].wait()
-            taken.add(own)
-        if (part, j) not in taken:
-            core_copies[part, j].wait_recv()
-            core_send()
-            taken.add((part, j))
-
-    place = {4: 0, 3: 1, 5: 2, 2: 3, 6: 4, 1: 5, 7: 6, 0: 7}
-
-    def z_at(p):
-        return zj(4 + lax.div(p + 1, 2) * (2 * lax.rem(p + 1, 2) - 1))
-
-    def chip_sum_b(j, first=0, n=8):
-        take("m", "b", j)
+            at = cols(640 * other, 640)
+            pairs = [(gv.at[zj(j), :, :, at], got_v.at[j]), (ga.at[zj(j), :, :, at], got_a.at[j])]
+        core_copies[piece] = [send(src, dst, core) for src, dst in pairs]
+
+    def take(own, *piece):
+        for name in own:
+            if name not in taken:
+                own_copies[name].wait()
+                taken.add(name)
+        for copy in core_copies[piece]:
+            copy.wait_recv()
+        core_send()
+
+    def chip_sum_b(j, *blocks):
+        take("m", "b", j, *blocks)
+        first, n = blocks or (0, 8)
         yy = yj(j)
         high, low = lax.div(yy, 2), lax.rem(yy, 2) * 1024
 
@@ -158,8 +170,9 @@
 
         lax.fori_loop(first, first + n, body, 0)
 
-    def chip_sum_c(j, first=0, n=8):
-        take("m", "c", j)
+    def chip_sum_c(j, *blocks):
+        take("m", "c", j, *blocks)
+        first, n = blocks or (0, 8)
         at = cols(2048 + xj(j) * 512, 512)
 
         def body(p, _):
@@ -171,9 +184,10 @@
         lax.fori_loop(first, first + n, body, 0)
 
     def chip_sum_a(j):
+        take("va", "a", j)
         zz = zj(j)
-        sum_a[j, :, :, 0:640] = own_v[zz].astype(f32) + got_v[zz].astype(f32)
-        sum_a[j, :, :, 640:1280] = own_a[zz].astype(f32) + got_a[zz].astype(f32)
+        sum_a[j, :, :, 0:640] = own_v[zz].astype(f32) + got_v[j].astype(f32)
+        sum_a[j, :, :, 640:1280] = own_a[zz].astype(f32) + got_a[j].astype(f32)
 
     class Ring4:
         def __init__(self, piece, r2, l2, from_l, from_r, right, left):
@@ -261,12 +275,17 @@
     ring_a = Ring8(columns_a(sum_a), columns_a(rm_a), columns_a(lm_a))
     ring_b, ring_c = ring8(sum_b, rm_b, lm_b), ring8(sum_c, rm_c, lm_c)
 
-    for _ in range(4):
+    for _ in range(6):
         core_send()
+    chip_sum_a(4)
+    ring_a.first()
     chip_sum_b(2, 0, 3)
     rb[0].far()
     chip_sum_c(2, 0, 3)
     rc[0].far()
+    chip_sum_a(3)
+    chip_sum_a(5)
+    ring_a.second()
     chip_sum_b(2, 3, 5)
     rb[1].far()
     chip_sum_c(2, 3, 5)
@@ -282,15 +301,9 @@
     for ring in (rb[1], rc[1]):
         ring.near_right()
         ring.near_left()
-    take("v", "v", 0)
-    take("a", "a", 0)
-    chip_sum_a(4)
-    ring_a.first()
+    ring_a.step(3, 0)
     rb[0].pass_on()
     rc[0].pass_on()
-    chip_sum_a(3)
-    chip_sum_a(5)
-    ring_a.second()
 
     def first_sends(ring):
         ring.far()
@@ -301,24 +314,16 @@
     first_sends(rc[2])
     chip_sum_a(2)
     chip_sum_a(6)
-    chip_sum_b(0)
-    chip_sum_c(0)
-    ring_a.step(3, 0)
+    ring_a.step(2, 1)
     rb[1].pass_on()
     rc[1].pass_on()
     first_sends(rb[3])
     first_sends(rc[3])
-    rb[0].end()
-    ring_b.first()
-    ring_b.second()
-    rc[0].end()
-    ring_c.first()
-    ring_c.second()
+    chip_sum_b(0)
+    chip_sum_c(0)
     chip_sum_a(1)
     chip_sum_a(7)
-    chip_sum_a(0)
-    ring_a.step(2, 1)
-
+    ring_a.step(2, 0)
     col_a, col_b, col_c = yl * 640, yl * 1024 + x * 256, 2048 + x * 512 + yl * 256
     mine, theirs = pl.ds(pl.multiple_of(c * 8, 8), 8), pl.ds(pl.multiple_of(other * 8, 8), 8)
     inputs = ((mv, ma, ml), (nv, na, nl), (sv, sa, sl))
@@ -337,36 +342,43 @@
     for k, (v, a, m) in enumerate(inputs):
         state_copies += [load(v, state_v.at[k]), load(a, state_a.at[k]), load(m, state_m.at[k])]
 
+    rb[0].end()
+    ring_b.first()
+    ring_b.second()
+    rc[0].end()
+    ring_c.first()
+    ring_c.second()
+    ring_a.step(1, 1)
+    chip_sum_a(0)
     rb[2].pass_on()
     rc[2].pass_on()
-    ring_a.step(2, 0)
-    rb[1].end()
-    ring_b.step(3, 0)
-    ring_b.step(2, 1)
-    rc[1].end()
-    ring_c.step(3, 0)
-    ring_c.step(2, 1)
-    ring_a.step(1, 1)
     rb[3].pass_on()
     rc[3].pass_on()
+    rb[1].end()
+    rc[1].end()
+    ring_b.step(3, 0)
+    ring_c.step(3, 0)
+    ring_a.step(1, 0)
+    ring_b.step(2, 1)
+    ring_c.step(2, 1)
     rb[2].end()
     rc[2].end()
+    ring_b.step(2, 0)
+    ring_c.step(2, 0)
     ring_b.step(1, 1)
     ring_c.step(1, 1)
-    ring_b.step(2, 0)
-    ring_c.step(2, 0)
-    ring_a.step(1, 0)
     rb[3].end()
     rc[3].end()
-    ring_b.step(1, 0)
-    ring_c.step(1, 0)
-
+
+    past = seen()
     ring_a.end(lambda h: a1.at[:, :, pl.ds(640 * h, 640)])
     a2_copies = []
     for k in range(1, 4):
         yy = yj(k)
         src = a1.at[lax.div(yy, 2), :, cols(lax.rem(yy, 2) * 640, 640)]
         a2_copies.append(send(src, a2_got.at[k - 1], device(x, yy, z, c)))
+    ring_b.step(1, 0)
+    ring_c.step(1, 0)
 
     def owned(ref, i):
         return ref.at[lax.div(i, 2), :, cols(lax.rem(i, 2) * 256, 256)]
@@ -404,11 +416,13 @@
     update_owned(b2, x, b3_got, b3_copies, col_b, st_b, new_b)
     at = pm.at[z, yh, :, cols(4096 * c + col_b, 256)]
     own_b = load(new_b, at)
-    xb_copies = [send(new_b, at, device(xj(k), y, z, c)) for k in (2, 1, 3)]
+    b_z = {(8 - k) % 8: send(new_b, at, device(x, y, zj(k), c)) for k in (1, 7, 2, 6, 3, 5, 4)}
+    b_last = {0: [send(new_b, at, device(xj(k), y, z, c)) for k in (2, 1, 3)]}
     update_owned(c2, y, c3_got, c3_copies, col_c, st_c, new_c)
     at = pm.at[z, yh, :, cols(4096 * c + col_c, 256)]
     own_c = load(new_c, at)
-    yc_copies = [send(new_c, at, device(x, yj(k), z, c)) for k in (2, 1, 3)]
+    c_z = {(8 - k) % 8: send(new_c, at, device(x, y, zj(k), c)) for k in (1, 7, 2, 6, 3, 5, 4)}
+    c_last = {0: [send(new_c, at, device(x, yj(k), z, c)) for k in (2, 1, 3)]}
     for copy in a3_copies:
         copy.wait_recv()
     total = (a3_all[0] + a3_all[1]) + (a3_all[2] + a3_all[3])
@@ -467,87 +481,70 @@
             return all_a.at[zz]
         return all_a.at[zz, :, :, pl.ds(640 * h, 640)]
 
-    class Block8:
-        def __init__(self, at):
-            self.at = at
-
-        def start(self):
-            own = self.at(z, None)
-            self.r1, self.l1 = send(own, own, right_z), send(own, own, left_z)
-            self.r2 = send(own, own, device(x, y, zj(2), c))
-            self.l2 = send(own, own, device(x, y, zj(6), c))
-
-        def near(self):
-            self.r1.wait_recv()
-            self.l1.wait_recv()
-
-        def pass_on(self):
-            self.r2.wait_recv()
-            at, part = self.at(zj(6), None), self.at(zj(6), 0)
-            self.r3 = send(at, at, right_z)
-            self.r4 = send(part, part, device(x, y, zj(2), c))
-            self.l2.wait_recv()
-            at, part = self.at(zj(2), None), self.at(zj(2), 1)
-            self.l3 = send(at, at, left_z)
-            self.l4 = send(part, part, device(x, y, zj(6), c))
-
-        def third(self):
-            self.r3.wait_recv()
-            self.l3.wait_recv()
-
-        def fourth(self):
-            self.r4.wait_recv()
-            self.l4.wait_recv()
-
     outs = []
 
     def put(at):
         outs.append(send(at, at, core))
 
-    def put_a(ref, first):
-        src, dst = all_a.at[:, :, :, pl.ds(first, 640)], ref.at[:, :, :, cols(640 * c, 640)]
-        outs.append(load(src, dst))
-        outs.append(send(src, dst, core))
+    def put_a(zz):
+        for ref, first in ((pv, 0), (pa, 640)):
+            src, dst = all_a.at[zz, :, :, pl.ds(first, 640)], ref.at[zz, :, :, cols(640 * c, 640)]
+            outs.append(load(src, dst))
+            outs.append(send(src, dst, core))
 
     def put_b(yy):
         put(pm.at[:, lax.div(yy, 2), :, cols(4096 * c + lax.rem(yy, 2) * 1024, 1024)])
 
     gather_a = Gather8(at_a8)
-    gather_b, gather_c = Block8(lambda zz, h: at_b(y, zz, h)), Block8(lambda zz, h: at_c(x, zz, h))
     by = [Relay4(lambda i, m=m: at_b(i, zj(m)), right_y, left_y, y, m < 4) for m in range(8)]
     cx = [Relay4(lambda i, m=m: at_c(i, zj(m)), right_x, left_x, x, m < 4) for m in range(8)]
-
-    def relays_start(*ms):
-        for relays in (by, cx):
-            for m in ms:
-                relays[m].start()
 
     def relays_pass(*ms):
         for relays in (by, cx):
             for m in ms:
                 relays[m].pass_on()
-
+        for relays, at, places in ((by, at_b, yj), (cx, at_c, xj)):
+            for m in ms:
+                relays[m].wait_near()
+                put(at(places(1), zj(m)))
+                put(at(places(3), zj(m)))
+
+    def spread(*ms):
+        for m in ms:
+            b_z[m].wait_recv()
+            at = pm.at[zj(m), yh, :, cols(4096 * c + col_b, 256)]
+            b_last[m] = [send(at, at, device(xj(k), y, z, c)) for k in (2, 1, 3)]
+            c_z[m].wait_recv()
+            at = pm.at[zj(m), yh, :, cols(4096 * c + col_c, 256)]
+            c_last[m] = [send(at, at, device(x, yj(k), z, c)) for k in (2, 1, 3)]
+
+    def whole(*ms):
+        for m in ms:
+            for copy in b_last[m]:
+                copy.wait_recv()
+            by[m].start()
+            for copy in c_last[m]:
+                copy.wait_recv()
+            cx[m].start()
+
+    spread(1, 7)
     own_b.wait()
-    for copy in xb_copies:
-        copy.wait_recv()
-    by[0].start()
-    gather_b.start()
     own_c.wait()
-    for copy in yc_copies:
-        copy.wait_recv()
-    cx[0].start()
-    gather_c.start()
+    whole(0)
+    spread(2, 6)
     for copy in ya_copies:
         copy.wait_recv()
     gather_a.start()
-    gather_b.near()
-    gather_c.near()
-    relays_start(1, 7)
-    gather_b.pass_on()
-    gather_c.pass_on()
-    relays_start(2, 6)
+    put_a(z)
+    drain(past)
+    past = seen()
+    spread(3, 5, 4)
+    whole(1, 7)
+    whole(2, 6)
     relays_pass(0)
     gather_a.pass_on(1)
+    put_a(zj(7))
+    put_a(zj(1))
     at_ta, at_tb, at_tc = (totals.at[:, cols(o, w)] for o, w in ((col_a, 640), (1280 + col_b, 256), (1280 + col_c, 256)))
     total_copies = [send(at_ta, at_ta, device(x, y_twin, z, c))]
     for k in range(4):
@@ -556,20 +553,23 @@
                 total_copies.append(send(at_tb, at_tb, device(xj(k), yy, z, c)))
                 total_copies.append(send(at_tc, at_tc, device(xj(k), yy, z, c)))
     relays_pass(1, 7)
-    gather_b.third()
-    gather_c.third()
-    relays_start(3, 5)
-    gather_b.fourth()
-    gather_c.fourth()
-    relays_start(4)
+    drain(past)
+    past = seen()
+    whole(3, 5, 4)
     put_b(y)
     put(at_c(x, slice(None)))
+    gather_a.pass_on(2)
+    put_a(zj(6))
+    put_a(zj(2))
     relays_pass(2, 6)
-    gather_a.pass_on(2)
     relays_pass(3, 5)
+    gather_a.pass_on(3)
+    put_a(zj(5))
+    put_a(zj(3))
     relays_pass(4)
-    gather_a.pass_on(3)
-
+
+    drain(past)
+    past = seen()
     for copy in total_copies:
         copy.wait_recv()
     row_copies = []
@@ -577,12 +577,6 @@
         at = out.at[:, cols(width * c, width)]
         row_copies.append(load(totals.at[mine, pl.ds(first, width)], at))
         row_copies.append(send(totals.at[theirs, pl.ds(first, width)], at, core))
-    for relay in by + cx:
-        relay.wait_near()
-    put_b(yj(1))
-    put_b(yj(3))
-    put(at_c(xj(1), slice(None)))
-    put(at_c(xj(3), slice(None)))
     for copy in row_copies:
         if copy.is_remote:
             copy.wait_recv()
@@ -605,21 +599,20 @@
     new_states = ((mv_out, ma_out, ml_out), (nv_out, na_out, nl_out), (sv_out, sa_out, sl_out))
     for k, (v, a, m) in enumerate(new_states):
         outs += [load(state_v.at[k], v), load(state_a.at[k], a), load(state_m.at[k], m)]
+    drain(past)
     for m in (0, 1, 7, 2, 6, 3, 5, 4):
         by[m].far.wait_recv()
         put(at_b(yj(2), zj(m)))
         cx[m].far.wait_recv()
         put(at_c(xj(2), zj(m)))
     gather_a.wait()
-    put_a(pv, 0)
-    put_a(pa, 640)
+    put_a(zj(4))
     for copy in outs:
         if copy.is_remote:
             copy.wait_recv()
         else:
             copy.wait()
-    for wait_send in started:
-        wait_send()
+    drain(seen())
 
 
 def whole_step(grads, states, step_counts):
@@ -659,7 +652,10 @@
 def copy_kernel(*refs):
     n = len(refs) // 2
     sems = refs[-1]
-    copies = [pltpu.make_async_copy(refs[k], refs[n + k], sems.at[k]) for k in range(n)]
+    pairs = list(zip(refs[:n], refs[n:-1]))
+    src, dst = pairs.pop(2)
+    pairs = [(src.at[pl.ds(k, 2)], dst.at[pl.ds(k, 2)]) for k in (0, 2, 4, 6)] + pairs
+    copies = [pltpu.make_async_copy(src, dst, sems.at[k]) for k, (src, dst) in enumerate(pairs)]
     for copy in copies:
         copy.start()
     for copy in copies:
@@ -674,7 +670,7 @@
         out_shape=[pltpu.HBM(a.shape, a.dtype) for a in arrays],
         in_specs=[anywhere] * n,
         out_specs=[anywhere] * n,
-        scratch_shapes=[pltpu.SemaphoreType.DMA((n,))],
+        scratch_shapes=[pltpu.SemaphoreType.DMA((n + 3,))],
         compiler_params=pltpu.CompilerParams(vmem_limit_bytes=2**20),
         name="copy_out",
     )(*[pltpu.with_memory_space_constraint(a, pltpu.VMEM) for a in arrays])

time: 81.8 us -> 77.6 us (0.949)
  Pallas kernels: 81 us -> 76.8 us
    pallas_call x1, Pallas kernels: 78.1 us -> 74 us  [whole_step(): pl.pallas_call(step_kernel, out_shape=[pltpu.VMEM(*s) for s in shapes], i...]
where the time goes in v3:
time: 77.6 us; the launch traced here: 77.5 us
  Pallas kernels  76.8 us (99%)
    pallas_call x1, Pallas kernels, whole_step(): pl.pallas_call(step_kernel, out_shape=[pltpu.VMEM(*s) for s in shapes], i...  74 us
    pallas_call x1, Pallas kernels, copy_out(): pl.pallas_call(copy_kernel, out_shape=[pltpu.HBM(a.shape, a.dtype) for a...  2.85 us

profile of v3, /device:TPU:1, one launch (start us, length us, event | category | flops | bytes accessed | tf_op | source)
XLA Modules:
  0.0 77.5 jit_solution(11453167570531034989)
XLA Ops:
  0.6 74.0 %sum_update_gather.1 = (bf16[8,2,16,1280]{3,2,1,0:T(8,128)(2,1)S(1)}, bf16[8,2,16,1280]{3,2,1,0:T(8,128)(2,1)S(1)}, bf16[8,2,16,8192]{3,2,1,0:T(8,128)(2,1)S(1)}...) custom-call(bf16[8,2,16,1280]{3,2,1,0:T(8,128)(2,1)} %bitcast.7, ...), custom_call_target="tpu_custom_call" | custom-call | tf_op jit(solution)/shard_map/sum_update_gather/pallas_call | solution.py:639
  74.6 2.9 %copy_out.1 = (bf16[8,2,16,1280]{3,2,1,0:T(8,128)(2,1)}, bf16[8,2,16,1280]{3,2,1,0:T(8,128)(2,1)}, bf16[8,2,16,8192]{3,2,1,0:T(8,128)(2,1)}, f32[8,1280]{1,0:T(8...) custom-call(bf16[8,2,16,1280]{3,2,1,0:T(8,128)(2,1)S(1)} %get-tuple-, ...), custom_call_target="tpu_custom_call" | custom-call | tf_op jit(solution)/shard_map/copy_out/pallas_call | solution.py:668

commit v4 on v3

--- a/solution.py
+++ b/solution.py
@@ -577,6 +577,11 @@
         at = out.at[:, cols(width * c, width)]
         row_copies.append(load(totals.at[mine, pl.ds(first, width)], at))
         row_copies.append(send(totals.at[theirs, pl.ds(first, width)], at, core))
+    for m in (0, 1, 7, 2, 6):
+        by[m].far.wait_recv()
+        put(at_b(yj(2), zj(m)))
+        cx[m].far.wait_recv()
+        put(at_c(xj(2), zj(m)))
     for copy in row_copies:
         if copy.is_remote:
             copy.wait_recv()
@@ -600,7 +605,7 @@
     for k, (v, a, m) in enumerate(new_states):
         outs += [load(state_v.at[k], v), load(state_a.at[k], a), load(state_m.at[k], m)]
     drain(past)
-    for m in (0, 1, 7, 2, 6, 3, 5, 4):
+    for m in (3, 5, 4):
         by[m].far.wait_recv()
         put(at_b(yj(2), zj(m)))
         cx[m].far.wait_recv()

time: 77.6 us -> 77.6 us (level)
  no operation moved by 1% of the time
where the time goes in v4:
time: 77.6 us; the launch traced here: 77.5 us
  Pallas kernels  76.8 us (99%)
    pallas_call x1, Pallas kernels, whole_step(): pl.pallas_call(step_kernel, out_shape=[pltpu.VMEM(*s) for s in shapes], i...  74 us
    pallas_call x1, Pallas kernels, copy_out(): pl.pallas_call(copy_kernel, out_shape=[pltpu.HBM(a.shape, a.dtype) for a...  2.85 us

profile of v4, /device:TPU:1, one launch (start us, length us, event | category | flops | bytes accessed | tf_op | source)
XLA Modules:
  0.0 77.5 jit_solution(8831901545848495787)
XLA Ops:
  0.6 74.0 %sum_update_gather.1 = (bf16[8,2,16,1280]{3,2,1,0:T(8,128)(2,1)S(1)}, bf16[8,2,16,1280]{3,2,1,0:T(8,128)(2,1)S(1)}, bf16[8,2,16,8192]{3,2,1,0:T(8,128)(2,1)S(1)}...) custom-call(bf16[8,2,16,1280]{3,2,1,0:T(8,128)(2,1)} %bitcast.7, ...), custom_call_target="tpu_custom_call" | custom-call | tf_op jit(solution)/shard_map/sum_update_gather/pallas_call | solution.py:644
  74.6 2.9 %copy_out.1 = (bf16[8,2,16,1280]{3,2,1,0:T(8,128)(2,1)}, bf16[8,2,16,1280]{3,2,1,0:T(8,128)(2,1)}, bf16[8,2,16,8192]{3,2,1,0:T(8,128)(2,1)}, f32[8,1280]{1,0:T(8...) custom-call(bf16[8,2,16,1280]{3,2,1,0:T(8,128)(2,1)S(1)} %get-tuple-, ...), custom_call_target="tpu_custom_call" | custom-call | tf_op jit(solution)/shard_map/copy_out/pallas_call | solution.py:673
